TPU v7x, 512 devices: a whole 4x4x16 slice. The times are simulated.
512 devices in a mesh: users: 32 (over y, x, core), items: 16 (over z).
Axes of the slice: x: 4, y: 4, z: 16, core: 2. Of those that a mesh axis runs over, the one named last changes fastest.
Arguments:
- user_emb: bfloat16 [65536, 256], P('users'), may hold values from -0.375 to 0.375
- samples: int32 [512, 64], P('users'), may hold values from 0 to 127, as said below
- pos_item: int32 [65536], P('users'), may hold values from 0 to 16383
- item_feat: bfloat16 [16384, 1024], P(('items', 'users')), may hold values from -0.1875 to 0.1875
- tower_w: bfloat16 [1024, 256], replicated, may hold values from -5 to 5
- item_bias: bfloat16 [16384], P(('items', 'users')), may hold values from -4 to 352
Outputs:
- user_loss: float32 [65536], P('users')
- user_grad: float32 [65536, 256], P(('users', 'items'))
- weight_grad: float32 [1024, 256], replicated
Inputs may be any that keep to these rules, and one draw needn't show every extreme that they name: `samples`: each row lists 64 distinct cluster ids. Clusters k * 8 to (k + 1) * 8 - 1 form item shard k; at most 8 ids of one row fall in any one shard, and in every row some shard holds exactly 8 of them.
All inputs are finite; a program needn't handle non-finite values.
Results may differ from a plain program's by a relative error of at most 0.0036.
Values may be sent and summed in bfloat16 or wider, within the bound.
No kernel may reach another device: no remote copies, remote signals or barrier semaphores. Data moves between devices by JAX's collectives and lax.ppermute only.
A program may use at most 64 MiB of HBM per device.

v0:
```python
import jax
import jax.numpy as jnp
from jax import lax
from jax.sharding import PartitionSpec as P

CL = 128
BU = 128
PEAK = 8


NEG_FILL = -1e30


def body(user_emb, samples, pos_item, item_feat, tower_w, item_bias):
    shard_index = lax.axis_index("items")
    group_size = lax.axis_size("users")
    shard_rows = item_feat.shape[0] * group_size
    shard_clus = shard_rows // CL
    slot_count = min(PEAK, shard_clus)
    shard_feats, bias_rows = (
        lax.all_gather(item_feat, "users", axis=0, tiled=True),
        lax.all_gather(item_bias, "users", axis=0, tiled=True),
    )
    item_rows = jnp.dot(shard_feats, tower_w, preferred_element_type=jnp.float32).astype(
        jnp.bfloat16
    )
    emb_width = item_rows.shape[1]
    emb_tiles = item_rows.reshape(shard_clus, CL, emb_width)
    bias_float = bias_rows.astype(jnp.float32)
    bias_tiles = bias_float.reshape(shard_clus, CL)
    blocks = samples.shape[0]
    step_count = blocks // 4
    local_ids = samples - shard_index * shard_clus
    inside = (local_ids >= 0) & (local_ids < shard_clus)
    rank_in = jnp.cumsum(inside.astype(jnp.int32), axis=1) - 1
    slot_range = jnp.arange(slot_count, dtype=jnp.int32)
    matched = inside[:, None, :] & (rank_in[:, None, :] == slot_range[None, :, None])
    slot_ids = jnp.sum(jnp.where(matched, local_ids[:, None, :], 0), axis=2)
    slot_live = jnp.any(matched, axis=2)
    pos_local = pos_item - shard_index * shard_rows
    pos_live = (pos_local >= 0) & (pos_local < shard_rows)
    pos_index = jnp.clip(pos_local, 0, shard_rows - 1)
    pos_rows = item_rows[pos_index]
    pos_logit = (
        jnp.einsum("ud,ud->u", user_emb, pos_rows, preferred_element_type=jnp.float32)
        + bias_float[pos_index]
    )
    user_steps = user_emb.reshape(step_count, 4, BU, emb_width)
    slot_steps = slot_ids.reshape(step_count, 4, slot_count)
    live_steps = slot_live.reshape(step_count, 4, slot_count)
    pos_steps = pos_logit.reshape(step_count, 4, BU)
    plive_steps = pos_live.reshape(step_count, 4, BU)

    def scores_of(user_rows, cluster_ids, live_ids):
        picked = emb_tiles[cluster_ids]
        raw_scores = jnp.einsum(
            "gud,gkcd->gukc", user_rows, picked, preferred_element_type=jnp.float32
        )
        raw_scores = raw_scores + bias_tiles[cluster_ids][:, None]
        live_mask = jnp.broadcast_to(live_ids[:, None, :, None], raw_scores.shape)
        return (picked, jnp.where(live_mask, raw_scores, NEG_FILL), live_mask)

    def forward(inputs):
        user_rows, cluster_ids, live_ids, pos_part, pos_flag = inputs
        picked, raw_scores, live_mask = scores_of(user_rows, cluster_ids, live_ids)
        row_peak = jnp.maximum(
            jnp.max(raw_scores, axis=(2, 3)), jnp.where(pos_flag, pos_part, NEG_FILL)
        )
        exp_total = jnp.sum(
            jnp.where(live_mask, jnp.exp(raw_scores - row_peak[..., None, None]), 0.0), axis=(2, 3)
        )
        exp_total = exp_total + jnp.where(pos_flag, jnp.exp(pos_part - row_peak), 0.0)
        return (row_peak, exp_total)

    local_peak, local_total = lax.map(
        forward, (user_steps, slot_steps, live_steps, pos_steps, plive_steps)
    )
    local_peak = local_peak.reshape(-1)
    local_total = local_total.reshape(-1)
    pos_value = jnp.where(pos_live, pos_logit, 0.0)
    row_peak = lax.pmax(local_peak, "items")
    exp_total, pos_score = lax.psum(
        (local_total * jnp.exp(local_peak - row_peak), pos_value), "items"
    )
    log_total = row_peak + jnp.log(exp_total)
    user_loss = log_total - pos_score
    pos_weight = jnp.where(pos_live, jnp.exp(pos_logit - log_total) - 1.0, 0.0)

    def weights_of(user_rows, cluster_ids, live_ids, log_part):
        picked, raw_scores, live_mask = scores_of(user_rows, cluster_ids, live_ids)
        soft_weight = jnp.where(
            live_mask, jnp.exp(raw_scores - log_part[..., None, None]), 0.0
        ).astype(jnp.bfloat16)
        return (picked, soft_weight)

    def add_tiles(grad_tiles, user_rows, cluster_ids, live_ids, soft_weight):
        contrib = jnp.einsum(
            "gukc,gud->gkcd", soft_weight, user_rows, preferred_element_type=jnp.float32
        )
        contrib = jnp.where(live_ids[..., None, None], contrib, 0.0)
        return grad_tiles.at[cluster_ids.reshape(-1)].add(contrib.reshape(-1, CL, emb_width))

    def backward_both(grad_tiles, inputs):
        user_rows, cluster_ids, live_ids, log_part = inputs
        picked, soft_weight = weights_of(user_rows, cluster_ids, live_ids, log_part)
        grad_users = jnp.einsum(
            "gukc,gkcd->gud", soft_weight, picked, preferred_element_type=jnp.float32
        )
        return (add_tiles(grad_tiles, user_rows, cluster_ids, live_ids, soft_weight), grad_users)

    start_tiles = jnp.zeros((shard_clus, CL, emb_width), jnp.float32)
    scan_inputs = (user_steps, slot_steps, live_steps, log_total.reshape(step_count, 4, BU))
    pos_terms = pos_weight[:, None] * pos_rows.astype(jnp.float32)
    grad_tiles, grad_users = lax.scan(backward_both, start_tiles, scan_inputs)
    grad_users = grad_users.reshape(-1, emb_width) + pos_terms
    user_grad = lax.psum_scatter(grad_users, "items", scatter_dimension=0, tiled=True)
    grad_items = (
        grad_tiles.reshape(shard_rows, emb_width)
        .at[pos_index]
        .add(pos_weight[:, None] * user_emb.astype(jnp.float32))
    )
    contract = (((0,), (0,)), ((), ()))
    part_weight = lax.dot_general(
        shard_feats.astype(jnp.float32), grad_items, contract, precision=lax.Precision.HIGHEST
    )
    weight_grad = lax.psum(part_weight, ("users", "items"))
    return (user_loss, user_grad, weight_grad)


def solution(mesh):
    return jax.shard_map(
        body,
        mesh=mesh,
        in_specs=(
            P("users", None),
            P("users", None),
            P("users"),
            P(("items", "users"), None),
            P(),
            P(("items", "users")),
        ),
        out_specs=(P("users"), P(("users", "items"), None), P()),
        check_vma=False,
    )
```

profile of v0, /device:TPU:1, one launch (start us, length us, event | category | flops | bytes accessed | tf_op | source)
XLA Modules:
  0.0 819.7 jit_solution(18017372859213118122)
XLA Ops:
  7.2 0.7 all-gather.2.cloned.1.call-update
  8.0 0.7 fusion.21
  8.9 1.3 dynamic-slice
  10.9 0.8 dynamic-update-slice
  11.7 69.0 %all-reduce = bf16[1024]{0:T(1024)(128)(2,1)S(1)} all-reduce(bf16[1024]{0:T(1024)(128)(2,1)S(1)} %dynamic-update-slice), channel_id=1, replica_groups=mesh['users'=32,'items'=16] {'users'}, use_global_device_ids=true, to_apply=%add | all-reduce | flops 1024 | bytes 4096
  80.7 0.7 broadcast_clamp_fusion
  81.4 8.6 %gather_fusion.5 = f32[2048]{0:T(1024)S(1)} fusion(f32[1024]{0:T(1024)S(1)} %get-tuple-element.174, s32[2048]{0:T(1024)S(1)} %get-tuple-element.164), kind=kCustom, calls=%fused_computation.5 | custom fusion | bytes 24576 | tf_op jit(solution)/shard_map/gather | solution.py:46
  90.7 2.3 convolution_convert_fusion
  93.1 7.5 gather_fusion.4
  101.5 17.9 %while.24 = (s32[]{:T(128)}, f32[4,4,128]{2,1,0:T(4,128)S(1)}, f32[4,4,128]{2,1,0:T(4,128)S(1)}, pred[4,4,8]{2,1,0:T(4,128)(4,1)S(1)}, bf16[4,4,128,256]{3,2,1,0...) while((s32[]{:T(128)}, f32[4,4,128]{2,1,0:T(4,128)S(1)}, ...), condition=%wide.region_6.7_spmd, body=%wide.region_3.6_spmd.sunk | while | flops 272633440 | bytes 15036589 | solution.py:75
  102.9 1.9 fusion.43
  104.8 0.8 select_reduce_fusion.3
  106.7 0.7 gather_fusion.1
  107.4 1.9 fusion.43
  109.3 0.8 select_reduce_fusion.3
  111.8 1.9 fusion.43
  113.7 0.8 select_reduce_fusion.3
  116.3 1.9 fusion.43
  118.2 0.8 select_reduce_fusion.3
  119.4 24.6 %pmax.7 = f32[2048]{0:T(1024)S(1)} all-reduce(f32[2048]{0:T(1024)S(1)} %bitcast.148), channel_id=1, replica_groups=mesh['users'=32,'items'=16] {'items'}, use_global_device_ids=true, to_apply=%region_7.8 | all-reduce | flops 2048 | bytes 16384 | tf_op jit(solution)/shard_map/pmax | solution.py:81
  144.1 39.0 %all-reduce.1 = (f32[2048]{0:T(1024)S(1)}, f32[2048]{0:T(1024)S(1)}) all-reduce(f32[2048]{0:T(1024)S(1)} %exponential_multiply_fusion, f32[2048]{0:T(1024)S(1)} %get-tuple-element.161), channel_id=1, replica_groups=mesh['users'=32,'items'=16] {'items'}, use_global_device_ids=true, to_apply=%region_8.9 | all-reduce | flops 4096 | bytes 32768 | tf_op jit(solution)/shard_map/psum | solution.py:82
  183.2 64.0 %while.25 = (s32[]{:T(128)}, f32[8,128,256]{2,1,0:T(8,128)S(1)}, f32[4,4,128,256]{3,2,1,0:T(8,128)}, s32[4,4,8]{2,1,0:T(4,128)S(1)}, pred[4,4,8]{2,1,0:T(4,128)(...) while((s32[]{:T(128)}, f32[8,128,256]{2,1,0:T(8,128)S(1)}, ...), condition=%wide.region_12.13_spmd, body=%wide.region_10.12_spmd.sunk | while | flops 810026176 | bytes 42005372 | solution.py:114
  184.0 2.0 gather_fusion.2
  186.0 2.6 select_convert_fusion.2
  188.7 1.3 fusion.52
  190.0 2.8 convolution_select_fusion.2
  192.7 6.5 scatter_fusion
  200.0 2.0 gather_fusion.2
  202.0 2.6 select_convert_fusion.2
  204.7 1.3 fusion.52
  206.0 2.8 convolution_select_fusion.2
  208.7 6.4 scatter_fusion
  216.0 2.0 gather_fusion.2
  218.1 2.6 select_convert_fusion.2
  220.7 1.3 fusion.52
  221.9 2.8 convolution_select_fusion.2
  224.7 6.5 scatter_fusion
  232.0 2.0 gather_fusion.2
  234.0 2.6 select_convert_fusion.2
  236.7 1.3 fusion.52
  238.0 2.8 convolution_select_fusion.2
  240.7 6.4 scatter_fusion
  247.2 15.9 %scatter_custom_fusion.1 = f32[1024,256]{1,0:T(8,128)S(1)} fusion(f32[1024,256]{1,0:T(8,128)S(1)} %bitcast.128, s32[2048]{0:T(1024)S(1)} %get-tuple-element.165, bf16[2048,256]{1,0:T(8,128)(2,1)} %bitcast.137, f32[2048]{0:T(1024)S(1)} %get-tuple-element.159), kind=kCustom, calls=%fused_computation.46 | custom fusion | flops 1572864 | bytes 2105344 | tf_op jit(solution)/shard_map/scatter-add | solution.py:120
  263.1 4.5 convolution_bitcast_fusion.1
  267.7 3.3 fusion.17
  271.6 478.1 %all-reduce.4.cloned.1.call-done = f32[1024,256]{0,1:T(8,128)} async-done(((f32[1024,256]{0,1:T(8,128)}), f32[1024,256]{0,1:T(8,128)}) %all-reduce.4.cloned.1.call-update) | async-done | bytes 1048592 | tf_op jit(solution)/shard_map/psum | solution.py:126
  749.7 2.5 copy.14
  752.2 61.0 %reduce-scatter.2.cloned.1.call-done = f32[128,256]{1,0:T(8,128)} async-done(((f32[2048,256]{1,0:T(8,128)}), f32[128,256]{1,0:T(8,128)}) %reduce-scatter.2.cloned.1.call-update) | async-done | bytes 131088 | tf_op jit(solution)/shard_map/reduce_scatter | solution.py:116
  (118 shorter events, 12.4 us)
Async XLA Ops:
  7.2 83.6 %copy-start = (bf16[1024,256]{1,0:T(8,128)(2,1)S(1)}, bf16[1024,256]{1,0:T(8,128)(2,1)}, u32[]{:S(2)}) copy-start(bf16[1024,256]{1,0:T(8,128)(2,1)} %param.14) | copy-start | bytes 1572868
  7.2 83.5 %all-gather.2.cloned.1.call-start = ((), (), s32[]{:S(2)}) async-start(), calls=%async_computation.1 | async-start | bytes 2162688 | tf_op jit(solution)/shard_map/all_gather | solution.py:21
  7.9 741.7 %all-reduce.4.cloned.1.call-start = ((), (), s32[]{:S(2)}) async-start(), calls=%async_computation.3 | async-start | bytes 2097152 | tf_op jit(solution)/shard_map/psum | solution.py:126
  93.0 7.5 copy-start.2
  100.6 1.0 copy-start.5
  100.6 0.7 copy-start.7
  104.8 1.2 copy-start.3
  109.2 1.2 copy-start.3
  113.7 1.2 copy-start.3
  118.2 1.2 copy-start.3
  184.0 2.0 copy-start.4
  186.0 2.6 copy-start.1
  200.0 2.0 copy-start.4
  202.0 2.6 copy-start.1
  216.0 2.0 copy-start.4
  218.0 2.6 copy-start.1
  232.0 2.0 copy-start.4
  234.0 2.6 copy-start.1
  263.1 4.6 copy-start.6
  267.6 545.6 %reduce-scatter.2.cloned.1.call-start = ((), (), s32[]{:S(2)}) async-start(), calls=%async_computation.2 | async-start | bytes 2228224 | tf_op jit(solution)/shard_map/reduce_scatter | solution.py:116
Sparse Core Ops, SparseCore 0:
  11.1 64.8 all-gather.1
  267.7 481.8 all-reduce.3
  753.1 60.0 reduce-scatter.1
where the time goes:
time: 830 us; the launch traced here: 820 us
  waiting for transfers between devices  540 us (65%)
  blocking collectives  133 us (16%)
  other arithmetic  51.7 us (6%)
  matrix products  40.9 us (5%)
  local copies, waits for them, and re-layouts  39.6 us (5%)
  between operations  14.6 us (2%)
    psum x1, waiting for transfers between devices, body(): weight_grad = lax.psum(part_weight, ('users', 'items'))  478 us
    unnamed x1, blocking collectives  69 us
    reduce_scatter x1, waiting for transfers between devices, body(): lax.psum_scatter(grad_users, 'items', scatter_dimension=0, tiled=True)  61 us
    psum x1, blocking collectives, body(): lax.psum((local_total * jnp.exp(local_peak - row_peak), pos_value), 'items')  39 us
    scatter-add x4, other arithmetic, add_tiles(): grad_tiles.at[cluster_ids.reshape(-1)]  25.8 us
    pmax x1, blocking collectives, body(): row_peak = lax.pmax(local_peak, 'items')  24.6 us
    dot_general x8, matrix products, scores_of(): jnp.einsum('gud,gkcd->gukc', user_rows, picked, preferred_element_type=jn...  17.9 us
  transfers between devices with their start and end apart: 3, of which 2 were waited for; matrix products, arithmetic and copies ran while one was open for 2% of the time, Pallas kernels for 0%

commit v1 on v0

v1 whole, which is shorter than its diff:
```python
import jax
import jax.numpy as jnp
from jax import lax
from jax.experimental import pallas as pl
from jax.experimental.pallas import tpu as pltpu
from jax.sharding import PartitionSpec as P

CL = 128
BU = 128
STEP = 256
NEG = -1e30
FLOOR = -1e29
NT = (((1,), (1,)), ((), ()))
f32 = jnp.float32
bf16 = jnp.bfloat16


def spread(x, axis, n):
    return lax.all_to_all(jnp.broadcast_to(x[None], (n,) + x.shape), axis, 0, 0)


def logits_of(item_ref, user_ref, mask_ref):
    width = user_ref.shape[1]
    raw = lax.dot_general(item_ref[:, :width], user_ref[...], NT, preferred_element_type=f32)
    bias = item_ref[:, width:].astype(f32)
    raw = raw + jnp.concatenate([bias] * (STEP // CL), axis=1)
    parts = [raw[c * CL : (c + 1) * CL] + mask_ref[c : c + 1, :] for c in range(raw.shape[0] // CL)]
    return raw, jnp.concatenate(parts, axis=0)


def at_positive(raw, pos_ref):
    return lax.broadcasted_iota(jnp.int32, raw.shape, 0) == pos_ref[...]


def forward(item_ref, user_ref, mask_ref, pos_ref, stat_ref):
    step = pl.program_id(0)
    raw, kept = logits_of(item_ref, user_ref, mask_ref)
    here = (pos_ref[...] >= 0) & (pos_ref[...] < raw.shape[0])
    pos = jnp.sum(jnp.where(at_positive(raw, pos_ref), raw, 0.0), axis=0, keepdims=True)
    pos = jnp.where(here, pos, NEG)
    peak = jnp.maximum(jnp.maximum(jnp.max(kept, axis=0, keepdims=True), pos), FLOOR)
    total = jnp.sum(jnp.exp(kept - peak), axis=0, keepdims=True) + jnp.exp(pos - peak)
    lse = jnp.where(total > 0.0, peak + jnp.log(jnp.maximum(total, 1e-37)), NEG)
    blocks = stat_ref.shape[0] // 2
    for h in range(STEP // BU):
        row = step * (STEP // BU) + h
        stat_ref[pl.ds(row, 1), :] = lse[:, h * BU : (h + 1) * BU]
        stat_ref[pl.ds(blocks + row, 1), :] = pos[:, h * BU : (h + 1) * BU]


def backward(item_ref, user_ref, mask_ref, pos_ref, stat_ref, grad_ref, high_ref, loss_ref, item_t, total_ref, weight_ref, sums):
    step = pl.program_id(0)
    width = user_ref.shape[1]
    blocks = loss_ref.shape[0]

    @pl.when(step == 0)
    def _():
        lse = stat_ref[:, :blocks, :]
        peak = jnp.max(lse, axis=0)
        total = peak + jnp.log(jnp.sum(jnp.exp(lse - peak[None]), axis=0))
        pos = jnp.max(stat_ref[:, blocks:, :], axis=0)
        total_ref[...] = total
        loss_ref[...] = total - pos
        weight_ref[...] = jnp.exp(pos - total) - 1.0
        item_t[...] = item_ref[:, :width].astype(f32).T.astype(bf16)
        sums[...] = jnp.zeros_like(sums)

    def row_of(ref):
        rows = [ref[pl.ds(step * (STEP // BU) + h, 1), :] for h in range(STEP // BU)]
        return jnp.concatenate(rows, axis=1)

    raw, kept = logits_of(item_ref, user_ref, mask_ref)
    soft = jnp.exp(kept - row_of(total_ref))
    soft = soft + jnp.where(at_positive(raw, pos_ref), row_of(weight_ref), 0.0)
    soft = soft.astype(bf16)
    sums[...] += jnp.dot(soft, user_ref[...], preferred_element_type=f32)
    grad_ref[...] = jnp.dot(item_t[...], soft, preferred_element_type=f32).T.astype(bf16)

    @pl.when(step == pl.num_programs(0) - 1)
    def _():
        high = sums[...].astype(bf16)
        high_ref[:, :width] = high
        high_ref[:, width:] = (sums[...] - high.astype(f32)).astype(bf16)


def body(user_emb, samples, pos_item, item_feat, tower_w, item_bias):
    group, shards = lax.axis_size("users"), lax.axis_size("items")
    shard = lax.axis_index("items")
    own, width = item_feat.shape[0], tower_w.shape[1]
    rows = own * group
    clus = rows // CL
    users, blocks = user_emb.shape[0], samples.shape[0]
    steps = users // STEP

    own_emb = jnp.dot(item_feat, tower_w, preferred_element_type=f32).astype(bf16)
    packed = jnp.concatenate([own_emb, jnp.broadcast_to(item_bias[:, None], (own, CL))], axis=1)
    items = spread(packed, "users", group).reshape(rows, width + CL)
    feats = lax.all_gather(item_feat, "users", axis=0, tiled=True)

    ids = shard * clus + jnp.arange(clus, dtype=jnp.int32)
    taken = jnp.any(samples[None] == ids[:, None, None], axis=2)
    mask = jnp.repeat(jnp.where(taken, 0.0, NEG).astype(f32), BU, axis=1)
    pos_row = (pos_item - shard * rows).reshape(1, users)

    in_specs = [
        pl.BlockSpec((rows, width + CL), lambda i: (0, 0)),
        pl.BlockSpec((STEP, width), lambda i: (i, 0)),
        pl.BlockSpec((clus, STEP), lambda i: (0, i)),
        pl.BlockSpec((1, STEP), lambda i: (0, i)),
    ]
    params = pltpu.CompilerParams(vmem_limit_bytes=40 << 20)
    stat = pl.pallas_call(
        forward,
        grid=(steps,),
        in_specs=in_specs,
        out_specs=pl.BlockSpec((2 * blocks, BU), lambda i: (0, 0)),
        out_shape=jax.ShapeDtypeStruct((2 * blocks, BU), f32),
        compiler_params=params,
    )(items, user_emb, mask, pos_row)
    stats = spread(stat, "items", shards)
    grad, high, loss = pl.pallas_call(
        backward,
        grid=(steps,),
        in_specs=in_specs + [pl.BlockSpec((shards, 2 * blocks, BU), lambda i: (0, 0, 0))],
        out_specs=[
            pl.BlockSpec((STEP, width), lambda i: (i, 0)),
            pl.BlockSpec((rows, 2 * width), lambda i: (0, 0)),
            pl.BlockSpec((blocks, BU), lambda i: (0, 0)),
        ],
        out_shape=[
            jax.ShapeDtypeStruct((users, width), bf16),
            jax.ShapeDtypeStruct((rows, 2 * width), bf16),
            jax.ShapeDtypeStruct((blocks, BU), f32),
        ],
        scratch_shapes=[
            pltpu.VMEM((width, rows), bf16),
            pltpu.VMEM((blocks, BU), f32),
            pltpu.VMEM((blocks, BU), f32),
            pltpu.VMEM((rows, width), f32),
        ],
        compiler_params=params,
    )(items, user_emb, mask, pos_row, stats)

    part = lax.dot_general(feats, high, (((0,), (0,)), ((), ())), preferred_element_type=f32)
    part = (part[:, :width] + part[:, width:]).astype(bf16)
    cut = part.shape[0] // group
    part = lax.all_to_all(part.reshape(group, cut, width), "users", 0, 0)
    part = jnp.sum(part.astype(f32), axis=0).astype(bf16)
    part = jnp.sum(spread(part, "items", shards).astype(f32), axis=0).astype(bf16)
    weight_grad = spread(part, "users", group).reshape(group * cut, width).astype(f32)

    grad = lax.all_to_all(grad.reshape(shards, users // shards, width), "items", 0, 0)
    user_grad = jnp.sum(grad.astype(f32), axis=0)
    return loss.reshape(users), user_grad, weight_grad


def solution(mesh):
    return jax.shard_map(
        body,
        mesh=mesh,
        in_specs=(
            P("users", None),
            P("users", None),
            P("users"),
            P(("items", "users"), None),
            P(),
            P(("items", "users")),
        ),
        out_specs=(P("users"), P(("users", "items"), None), P()),
        check_vma=False,
    )
```

time: 830 us -> 207 us (0.25); the launches traced: 820 us -> 207 us
  waiting for transfers between devices: 540 us -> 70.1 us
  blocking collectives: 133 us -> 67.5 us
  other arithmetic: 51.7 us -> 2.45 us
  matrix products: 40.9 us -> 3.88 us
  local copies, waits for them, and re-layouts: 39.6 us -> 3.22 us
  starting transfers between devices: 0.12 us -> 30.7 us
  Pallas kernels: 0 us -> 14.9 us
    psum x1 -> x0, waiting for transfers between devices: 478 us -> none  [body(): weight_grad = lax.psum(part_weight, ('users', 'items'))]
    all_to_all x0 -> x3, waiting for transfers between devices: none -> 69.4 us  [the longest x1 44.8 us: body(): lax.all_to_all(grad.reshape(shards, users // shards, width), 'items', 0, 0)]
    unnamed x1 -> x0, blocking collectives: 69 us -> none
    all_to_all x0 -> x3, blocking collectives: none -> 67.5 us  [the longest x2 46.9 us: spread(): return lax.all_to_all(jnp.broadcast_to(x[None], (n,) + x.shape), axis, 0, 0)]
    reduce_scatter x1 -> x0, waiting for transfers between devices: 61 us -> none  [body(): lax.psum_scatter(grad_users, 'items', scatter_dimension=0, tiled=True)]
    scatter-add x5 -> x0, other arithmetic: 41.7 us -> none  [the longest x4 25.8 us: add_tiles(): grad_tiles.at[cluster_ids.reshape(-1)]]
    psum x1 -> x0, blocking collectives: 39 us -> none  [body(): lax.psum((local_total * jnp.exp(local_peak - row_peak), pos_value), 'items')]
    dot_general x18 -> x2, matrix products: 40.9 us -> 3.88 us  [the longest x1 2.85 us: body(): lax.dot_general(feats, high, (((0,), (0,)), ((), ())), preferred_element_...]
  transfers between devices with their start and end apart: 3 -> 4, of which waited for: 2 -> 3; matrix products, arithmetic and copies ran while one was open for 2% -> 2% of each run, Pallas kernels for 0% -> 7%
where the time goes in v1:
time: 207 us
  waiting for transfers between devices  70.1 us (34%)
  blocking collectives  67.5 us (33%)
  starting transfers between devices  30.7 us (15%)
  Pallas kernels  14.9 us (7%)
  between operations  14.2 us (7%)
  matrix products  3.88 us (2%)
  local copies, waits for them, and re-layouts  3.22 us (2%)
  other arithmetic  2.45 us (1%)
    all_to_all x2, blocking collectives, spread(): return lax.all_to_all(jnp.broadcast_to(x[None], (n,) + x.shape), axis, 0, 0)  46.9 us
    all_to_all x1, waiting for transfers between devices, body(): lax.all_to_all(grad.reshape(shards, users // shards, width), 'items', 0, 0)  44.8 us
    all_to_all x2, waiting for transfers between devices, spread(): return lax.all_to_all(jnp.broadcast_to(x[None], (n,) + x.shape), axis, 0, 0)  24.6 us
    all_to_all x1, blocking collectives, body(): part = lax.all_to_all(part.reshape(group, cut, width), 'users', 0, 0)  20.6 us
    all_to_all x2, starting transfers between devices, spread(): return lax.all_to_all(jnp.broadcast_to(x[None], (n,) + x.shape), axis, 0, 0)  20.3 us
    all_to_all x1, starting transfers between devices, body(): lax.all_to_all(grad.reshape(shards, users // shards, width), 'items', 0, 0)  10.4 us
    pallas_call x1, Pallas kernels, body(): pl.pallas_call(backward, grid=(steps,), in_specs=in_specs + [pl.BlockSpec...  9.4 us
    pallas_call x1, Pallas kernels, body(): pl.pallas_call(forward, grid=(steps,), in_specs=in_specs, out_specs=pl.Bl...  5.46 us
  transfers between devices with their start and end apart: 4, of which 3 were waited for; matrix products, arithmetic and copies ran while one was open for 2% of the time, Pallas kernels for 7%

profile of v1, /device:TPU:1, one launch (start us, length us, event | category | flops | bytes accessed | tf_op | source)
XLA Modules:
  0.0 206.9 jit_solution(5697859861107389436)
XLA Ops:
  7.2 0.0 copy-start
  7.2 0.0 copy-start.2
  7.2 0.0 copy-start.3
  7.2 0.0 copy-start.1
  7.2 0.0 all-gather.2.cloned.1.call-start
  7.3 0.7 all-gather.2.cloned.1.call-update
  7.9 0.3 copy-done
  8.2 1.0 convolution_convert_fusion
  9.2 0.7 broadcast_in_dim.20
  10.0 1.0 broadcast_in_dim.21
  10.9 10.4 %all-to-all-start = ((bf16[32,32,384]{2,1,0:T(8,128)(2,1)}), bf16[32,32,384]{2,1,0:T(8,128)(2,1)S(1)}, u32[]{:S(2)}, u32[]{:S(2)}) async-start(bf16[32,32,384]{2,1,0:T(8,128)(2,1)} %broadcast_in_dim.21), calls=%async_computation | async-start | bytes 1572864 | tf_op jit(solution)/shard_map/all_to_all | solution.py:19
  21.4 0.0 copy-done.2
  21.4 0.3 compare_reduce_fusion
  21.7 0.1 copy.10
  21.8 0.0 copy-done.3
  21.8 0.1 broadcast_bitcast_fusion.mask_ref
  21.9 13.9 %all-to-all-done = bf16[32,32,384]{2,1,0:T(8,128)(2,1)S(1)} async-done(((bf16[32,32,384]{2,1,0:T(8,128)(2,1)}), bf16[32,32,384]{2,1,0:T(8,128)(2,1)S(1)}, u32[]{:S(2)}, u32[]{:S(2)}) %all-to-all-start) | async-done | bytes 786464 | tf_op jit(solution)/shard_map/all_to_all | solution.py:19
  35.7 0.0 copy-done.1
  35.7 5.5 %shard_map.85 = f32[32,128]{1,0:T(8,128)S(1)} custom-call(bf16[1024,384]{1,0:T(8,128)(2,1)S(1)} %bitcast.16, bf16[2048,256]{1,0:T(8,128)(2,1)S(1)} %copy-done.1, f32[8,2048]{1,0:T(8,128)S(1)} %broadcast_bitcast_fusion.mask_ref, s32[1,2048]{1,0:T(1,128)S(1)} %bitcast.18), custom_call_target="tpu_custom_call" | custom-call | tf_op jit(solution)/shard_map/pallas_call | solution.py:112
  41.2 26.2 %all_to_all.30.stat_ref = f32[16,32,128]{2,1,0:T(8,128)S(1)} all-to-all(f32[16,32,128]{2,1,0:T(8,128)S(1)} %broadcast_in_dim.25), channel_id=1, replica_groups=mesh['users'=32,'items'=16] {'items'}, dimensions={0} | all-to-all | bytes 524288 | tf_op jit(solution)/shard_map/all_to_all | solution.py:19
  67.4 9.4 %shard_map.86 = (bf16[2048,256]{1,0:T(8,128)(2,1)}, bf16[1024,512]{1,0:T(8,128)(2,1)S(1)}, f32[16,128]{1,0:T(8,128)}) custom-call(bf16[1024,384]{1,0:T(8,128)(2,1)S(1)} %bitcast.17, bf16[2048,256]{1,0:T(8,128)(2,1)S(1)} %copy-done.1, f32[8,2048]{1,0:T(8,128)S(1)} %broadcast_bitcast_fusion.mask_ref, s32[1,2048]{1,0:T(1,128)S(1)} %bitcast.19, ...), custom_call_target="tpu_custom_call" | custom-call | tf_op jit(solution)/shard_map/pallas_call | solution.py:121
  76.8 0.0 all-gather.2.cloned.1.call-done
  76.8 2.9 %convolution_bitcast_fusion = f32[1024,512]{0,1:T(8,128)S(1)} fusion(bf16[1024,512]{1,0:T(8,128)(2,1)S(1)} %get-tuple-element.8, bf16[1024,1024]{1,0:T(8,128)(2,1)} %all-gather.2.cloned.1.call-done), kind=kOutput, calls=%fused_computation.1 | convolution fusion | flops 1073741824 | bytes 5242880 | tf_op jit(solution)/shard_map/dot_general | solution.py:144
  79.7 0.1 fusion
  79.8 0.2 copy.11
  80.0 20.6 %all_to_all.31 = bf16[32,32,256]{2,1,0:T(8,128)(2,1)S(1)} all-to-all(bf16[32,32,256]{2,1,0:T(8,128)(2,1)S(1)} %bitcast.20), channel_id=1, replica_groups=mesh['users'=32,'items'=16] {'users'}, dimensions={0} | all-to-all | bytes 1048576 | tf_op jit(solution)/shard_map/all_to_all | solution.py:147
  100.7 0.1 reduce_sum.34
  100.8 20.7 %all_to_all.32 = bf16[16,32,256]{2,1,0:T(8,128)(2,1)S(1)} all-to-all(bf16[16,32,256]{2,1,0:T(8,128)(2,1)S(1)} %broadcast_in_dim.26), channel_id=1, replica_groups=mesh['users'=32,'items'=16] {'items'}, dimensions={0} | all-to-all | bytes 524288 | tf_op jit(solution)/shard_map/all_to_all | solution.py:19
  121.5 10.4 %all-to-all-start.2 = ((bf16[16,128,256]{2,1,0:T(8,128)(2,1)}), bf16[16,128,256]{2,1,0:T(8,128)(2,1)S(1)}, u32[]{:S(2)}, u32[]{:S(2)}) async-start(bf16[16,128,256]{2,1,0:T(8,128)(2,1)} %bitcast.4), calls=%async_computation.2 | async-start | bytes 2097152 | tf_op jit(solution)/shard_map/all_to_all | solution.py:152
  131.9 44.8 %all-to-all-done.2 = bf16[16,128,256]{2,1,0:T(8,128)(2,1)S(1)} async-done(((bf16[16,128,256]{2,1,0:T(8,128)(2,1)}), bf16[16,128,256]{2,1,0:T(8,128)(2,1)S(1)}, u32[]{:S(2)}, u32[]{:S(2)}) %all-to-all-start.2) | async-done | bytes 1048608 | tf_op jit(solution)/shard_map/all_to_all | solution.py:152
  176.7 0.9 broadcast_in_dim.50
  177.6 9.9 %all-to-all-start.5 = ((bf16[32,32,256]{2,1,0:T(8,128)(2,1)}), bf16[32,32,256]{2,1,0:T(8,128)(2,1)S(1)}, u32[]{:S(2)}, u32[]{:S(2)}) async-start(bf16[32,32,256]{2,1,0:T(8,128)(2,1)} %broadcast_in_dim.50), calls=%async_computation.5 | async-start | bytes 1048576 | tf_op jit(solution)/shard_map/all_to_all | solution.py:19
  187.4 0.8 convert_reduce_fusion
  188.2 10.8 %all-to-all-done.5 = bf16[32,32,256]{2,1,0:T(8,128)(2,1)S(1)} async-done(((bf16[32,32,256]{2,1,0:T(8,128)(2,1)}), bf16[32,32,256]{2,1,0:T(8,128)(2,1)S(1)}, u32[]{:S(2)}, u32[]{:S(2)}) %all-to-all-start.5) | async-done | bytes 524320 | tf_op jit(solution)/shard_map/all_to_all | solution.py:19
  199.0 1.1 bitcast_convert_fusion
  (7 shorter events, 0.1 us)
Async XLA Ops:
  7.2 1.0 copy-start
  7.2 14.2 %copy-start.2 = (s32[16,64]{1,0:T(8,128)S(1)}, s32[16,64]{1,0:T(8,128)}, u32[]{:S(2)}) copy-start(s32[16,64]{1,0:T(8,128)} %param.7) | copy-start | bytes 12292
  7.2 14.6 %copy-start.3 = (s32[2048]{0:T(1024)S(1)}, s32[2048]{0:T(1024)}, u32[]{:S(2)}) copy-start(s32[2048]{0:T(1024)} %param.8) | copy-start | bytes 24580
  7.2 28.5 %copy-start.1 = (bf16[2048,256]{1,0:T(8,128)(2,1)S(1)}, bf16[2048,256]{1,0:T(8,128)(2,1)}, u32[]{:S(2)}) copy-start(bf16[2048,256]{1,0:T(8,128)(2,1)} %user_ref.3) | copy-start | bytes 3145732
  7.2 69.6 %all-gather.2.cloned.1.call-start = ((), (), s32[]{:S(2)}) async-start(), calls=%async_computation.6 | async-start | bytes 2162688 | tf_op jit(solution)/shard_map/all_gather | solution.py:98
  10.9 24.8 %all-to-all-start = ((bf16[32,32,384]{2,1,0:T(8,128)(2,1)}), bf16[32,32,384]{2,1,0:T(8,128)(2,1)S(1)}, u32[]{:S(2)}, u32[]{:S(2)}) async-start(bf16[32,32,384]{2,1,0:T(8,128)(2,1)} %broadcast_in_dim.21), calls=%async_computation | async-start | bytes 1572864 | tf_op jit(solution)/shard_map/all_to_all | solution.py:19
  121.5 55.2 %all-to-all-start.2 = ((bf16[16,128,256]{2,1,0:T(8,128)(2,1)}), bf16[16,128,256]{2,1,0:T(8,128)(2,1)S(1)}, u32[]{:S(2)}, u32[]{:S(2)}) async-start(bf16[16,128,256]{2,1,0:T(8,128)(2,1)} %bitcast.4), calls=%async_computation.2 | async-start | bytes 2097152 | tf_op jit(solution)/shard_map/all_to_all | solution.py:152
  177.6 21.4 %all-to-all-start.5 = ((bf16[32,32,256]{2,1,0:T(8,128)(2,1)}), bf16[32,32,256]{2,1,0:T(8,128)(2,1)S(1)}, u32[]{:S(2)}, u32[]{:S(2)}) async-start(bf16[32,32,256]{2,1,0:T(8,128)(2,1)} %broadcast_in_dim.50), calls=%async_computation.5 | async-start | bytes 1048576 | tf_op jit(solution)/shard_map/all_to_all | solution.py:19
Sparse Core Ops, SparseCore 0:
  11.2 64.9 all-gather.1

commit v2 on v1

--- a/solution.py
+++ b/solution.py
@@ -48,7 +48,8 @@
         stat_ref[pl.ds(blocks + row, 1), :] = pos[:, h * BU : (h + 1) * BU]
 
 
-def backward(item_ref, user_ref, mask_ref, pos_ref, stat_ref, grad_ref, high_ref, loss_ref, item_t, total_ref, weight_ref, sums):
+def backward(shard_ref, item_ref, user_ref, mask_ref, pos_ref, stat_ref, *refs):
+    *grad_refs, high_ref, loss_ref, item_t, total_ref, weight_ref, sums = refs
     step = pl.program_id(0)
     width = user_ref.shape[1]
     blocks = loss_ref.shape[0]
@@ -74,7 +75,15 @@
     soft = soft + jnp.where(at_positive(raw, pos_ref), row_of(weight_ref), 0.0)
     soft = soft.astype(bf16)
     sums[...] += jnp.dot(soft, user_ref[...], preferred_element_type=f32)
-    grad_ref[...] = jnp.dot(item_t[...], soft, preferred_element_type=f32).T.astype(bf16)
+    grad = jnp.dot(item_t[...], soft, preferred_element_type=f32).T.astype(bf16)
+    span = len(grad_refs)
+    for h in range(STEP // BU):
+        away = lax.rem(step * (STEP // BU) + h - shard_ref[0] + span, span)
+        for shift, grad_ref in enumerate(grad_refs):
+
+            @pl.when(away == shift)
+            def _():
+                grad_ref[...] = grad[h * BU : (h + 1) * BU]
 
     @pl.when(step == pl.num_programs(0) - 1)
     def _():
@@ -118,17 +127,19 @@
         compiler_params=params,
     )(items, user_emb, mask, pos_row)
     stats = spread(stat, "items", shards)
-    grad, high, loss = pl.pallas_call(
+    *grads, high, loss = pl.pallas_call(
         backward,
         grid=(steps,),
-        in_specs=in_specs + [pl.BlockSpec((shards, 2 * blocks, BU), lambda i: (0, 0, 0))],
-        out_specs=[
-            pl.BlockSpec((STEP, width), lambda i: (i, 0)),
+        in_specs=[pl.BlockSpec(memory_space=pltpu.SMEM)]
+        + in_specs
+        + [pl.BlockSpec((shards, 2 * blocks, BU), lambda i: (0, 0, 0))],
+        out_specs=[pl.BlockSpec((BU, width), lambda i: (0, 0))] * shards
+        + [
             pl.BlockSpec((rows, 2 * width), lambda i: (0, 0)),
             pl.BlockSpec((blocks, BU), lambda i: (0, 0)),
         ],
-        out_shape=[
-            jax.ShapeDtypeStruct((users, width), bf16),
+        out_shape=[jax.ShapeDtypeStruct((BU, width), bf16)] * shards
+        + [
             jax.ShapeDtypeStruct((rows, 2 * width), bf16),
             jax.ShapeDtypeStruct((blocks, BU), f32),
         ],
@@ -139,7 +150,10 @@
             pltpu.VMEM((rows, width), f32),
         ],
         compiler_params=params,
-    )(items, user_emb, mask, pos_row, stats)
+    )(jnp.reshape(shard, (1,)), items, user_emb, mask, pos_row, stats)
+    for shift in range(1, shards):
+        pairs = [(k, (k + shift) % shards) for k in range(shards)]
+        grads[shift] = lax.ppermute(grads[shift], "items", pairs)
 
     part = lax.dot_general(feats, high, (((0,), (0,)), ((), ())), preferred_element_type=f32)
     part = (part[:, :width] + part[:, width:]).astype(bf16)
@@ -149,8 +163,7 @@
     part = jnp.sum(spread(part, "items", shards).astype(f32), axis=0).astype(bf16)
     weight_grad = spread(part, "users", group).reshape(group * cut, width).astype(f32)
 
-    grad = lax.all_to_all(grad.reshape(shards, users // shards, width), "items", 0, 0)
-    user_grad = jnp.sum(grad.astype(f32), axis=0)
+    user_grad = sum(grad.astype(f32) for grad in grads)
     return loss.reshape(users), user_grad, weight_grad
 
 

time: 207 us -> 240 us (1.16)
  starting transfers between devices: 30.7 us -> 91.7 us
  waiting for transfers between devices: 70.1 us -> 31.1 us
  local copies, waits for them, and re-layouts: 3.22 us -> 12.7 us
    ppermute x0 -> x15, starting transfers between devices: none -> 72.3 us  [body(): grads[shift] = lax.ppermute(grads[shift], 'items', pairs)]
    all_to_all x1 -> x0, waiting for transfers between devices: 44.8 us -> none  [body(): lax.all_to_all(grad.reshape(shards, users // shards, width), 'items', 0, 0)]
    ppermute x0 -> x15, waiting for transfers between devices: none -> 16.6 us  [body(): grads[shift] = lax.ppermute(grads[shift], 'items', pairs)]
    all_to_all x2, waiting for transfers between devices: 24.6 us -> 13.9 us  [spread(): return lax.all_to_all(jnp.broadcast_to(x[None], (n,) + x.shape), axis, 0, 0)]
    all_to_all x1 -> x0, starting transfers between devices: 10.4 us -> none  [body(): lax.all_to_all(grad.reshape(shards, users // shards, width), 'items', 0, 0)]
    unnamed x8 -> x68, local copies, waits for them, and re-layouts: 0.29 us -> 9.74 us
  transfers between devices with their start and end apart: 4 -> 18, of which waited for: 3 -> 6; matrix products, arithmetic and copies ran while one was open for 2% -> 2% of each run, Pallas kernels for 7% -> 7%
where the time goes in v2:
time: 240 us; the launch traced here: 239 us
  starting transfers between devices  91.7 us (38%)
  blocking collectives  66.4 us (28%)
  waiting for transfers between devices  31.1 us (13%)
  Pallas kernels  16 us (7%)
  between operations  14.6 us (6%)
  local copies, waits for them, and re-layouts  12.7 us (5%)
  matrix products  3.88 us (2%)
  other arithmetic  2.45 us (1%)
    ppermute x15, starting transfers between devices, body(): grads[shift] = lax.ppermute(grads[shift], 'items', pairs)  72.3 us
    all_to_all x2, blocking collectives, spread(): return lax.all_to_all(jnp.broadcast_to(x[None], (n,) + x.shape), axis, 0, 0)  45.6 us
    all_to_all x1, blocking collectives, body(): part = lax.all_to_all(part.reshape(group, cut, width), 'users', 0, 0)  20.8 us
    all_to_all x2, starting transfers between devices, spread(): return lax.all_to_all(jnp.broadcast_to(x[None], (n,) + x.shape), axis, 0, 0)  19.3 us
    ppermute x15, waiting for transfers between devices, body(): grads[shift] = lax.ppermute(grads[shift], 'items', pairs)  16.6 us
    all_to_all x2, waiting for transfers between devices, spread(): return lax.all_to_all(jnp.broadcast_to(x[None], (n,) + x.shape), axis, 0, 0)  13.9 us
    pallas_call x1, Pallas kernels, body(): pl.pallas_call(backward, grid=(steps,), in_specs=[pl.BlockSpec(memory_spa...  10.6 us
    unnamed x68, local copies, waits for them, and re-layouts  9.74 us
  transfers between devices with their start and end apart: 18, of which 6 were waited for; matrix products, arithmetic and copies ran while one was open for 2% of the time, Pallas kernels for 7%

profile of v2, /device:TPU:1, one launch (start us, length us, event | category | flops | bytes accessed | tf_op | source)
XLA Modules:
  0.0 238.9 jit_solution(9232815060696797374)
XLA Ops:
  7.3 0.7 all-gather.2.cloned.1.call-update
  8.2 1.0 convolution_convert_fusion
  9.2 0.7 broadcast_in_dim.20
  10.0 1.0 broadcast_in_dim.21
  10.9 10.4 %all-to-all-start = ((bf16[32,32,384]{2,1,0:T(8,128)(2,1)}), bf16[32,32,384]{2,1,0:T(8,128)(2,1)S(1)}, u32[]{:S(2)}, u32[]{:S(2)}) async-start(bf16[32,32,384]{2,1,0:T(8,128)(2,1)} %broadcast_in_dim.21), calls=%async_computation | async-start | bytes 1572864 | tf_op jit(solution)/shard_map/all_to_all | solution.py:19
  21.9 13.9 %all-to-all-done = bf16[32,32,384]{2,1,0:T(8,128)(2,1)S(1)} async-done(((bf16[32,32,384]{2,1,0:T(8,128)(2,1)}), bf16[32,32,384]{2,1,0:T(8,128)(2,1)S(1)}, u32[]{:S(2)}, u32[]{:S(2)}) %all-to-all-start) | async-done | bytes 786464 | tf_op jit(solution)/shard_map/all_to_all | solution.py:19
  35.7 5.4 %shard_map.85 = f32[32,128]{1,0:T(8,128)S(1)} custom-call(bf16[1024,384]{1,0:T(8,128)(2,1)S(1)} %bitcast.16, bf16[2048,256]{1,0:T(8,128)(2,1)S(1)} %copy-done.1, f32[8,2048]{1,0:T(8,128)S(1)} %broadcast_bitcast_fusion.mask_ref, s32[1,2048]{1,0:T(1,128)S(1)} %bitcast.18), custom_call_target="tpu_custom_call" | custom-call | tf_op jit(solution)/shard_map/pallas_call | solution.py:121
  41.2 26.2 %all_to_all.25.stat_ref = f32[16,32,128]{2,1,0:T(8,128)S(1)} all-to-all(f32[16,32,128]{2,1,0:T(8,128)S(1)} %broadcast_in_dim.25), channel_id=1, replica_groups=mesh['users'=32,'items'=16] {'items'}, dimensions={0} | all-to-all | bytes 524288 | tf_op jit(solution)/shard_map/all_to_all | solution.py:19
  67.4 10.6 %shard_map.86 = (bf16[128,256]{1,0:T(8,128)(2,1)S(1)}, bf16[128,256]{1,0:T(8,128)(2,1)S(1)}, bf16[128,256]{1,0:T(8,128)(2,1)S(1)}, bf16[128,256]{1,0:T(8,128)(2,...) custom-call(s32[1]{0:T(128)} %bitcast.shard_ref, ...), custom_call_target="tpu_custom_call" | custom-call | tf_op jit(solution)/shard_map/pallas_call | solution.py:130
  78.0 0.6 copy-done.2
  79.3 0.6 copy-done.6
  79.9 0.6 copy-done.8
  80.5 0.6 copy-done.10
  81.2 0.6 copy-done.12
  81.8 0.6 copy-done.14
  82.4 0.6 copy-done.16
  83.0 0.6 copy-done.18
  83.7 0.6 copy-done.20
  84.3 0.6 copy-done.22
  85.6 0.6 copy-done.26
  86.2 0.6 copy-done.28
  86.8 0.6 copy-done.30
  87.4 2.9 %convolution_bitcast_fusion = f32[1024,512]{0,1:T(8,128)S(1)} fusion(bf16[1024,512]{1,0:T(8,128)(2,1)S(1)} %get-tuple-element.38, bf16[1024,1024]{1,0:T(8,128)(2,1)} %all-gather.2.cloned.1.call-done), kind=kOutput, calls=%fused_computation | convolution fusion | flops 1073741824 | bytes 5242880 | tf_op jit(solution)/shard_map/dot_general | solution.py:158
  90.8 20.8 %all_to_all.26 = bf16[32,32,256]{2,1,0:T(8,128)(2,1)S(1)} all-to-all(bf16[32,32,256]{2,1,0:T(8,128)(2,1)S(1)} %bitcast.20), channel_id=1, replica_groups=mesh['users'=32,'items'=16] {'users'}, dimensions={0} | all-to-all | bytes 1048576 | tf_op jit(solution)/shard_map/all_to_all | solution.py:161
  111.8 19.4 %all_to_all.27 = bf16[16,32,256]{2,1,0:T(8,128)(2,1)S(1)} all-to-all(bf16[16,32,256]{2,1,0:T(8,128)(2,1)S(1)} %broadcast_in_dim.26), channel_id=1, replica_groups=mesh['users'=32,'items'=16] {'items'}, dimensions={0} | all-to-all | bytes 524288 | tf_op jit(solution)/shard_map/all_to_all | solution.py:19
  131.2 0.9 broadcast_in_dim.50
  132.0 8.9 %all-to-all-start.4 = ((bf16[32,32,256]{2,1,0:T(8,128)(2,1)}), bf16[32,32,256]{2,1,0:T(8,128)(2,1)S(1)}, u32[]{:S(2)}, u32[]{:S(2)}) async-start(bf16[32,32,256]{2,1,0:T(8,128)(2,1)} %broadcast_in_dim.50), calls=%async_computation.4 | async-start | bytes 1048576 | tf_op jit(solution)/shard_map/all_to_all | solution.py:19
  141.0 5.9 %collective-permute-start.14 = (bf16[128,256]{1,0:T(8,128)(2,1)S(1)}, bf16[128,256]{1,0:T(8,128)(2,1)S(1)}, u32[]{:S(2)}, u32[]{:S(2)}) collective-permute-start(bf16[128,256]{1,0:T(8,128)(2,1)S(1)} %copy-done.31), channel_id=1, source_target_pairs={{0,15},{1,0},{2,1},{3,2},{4,3},{5,4},{6,5},{7,6},{8,7},{9,8},{10,9... | collective-permute-start | bytes 196616 | tf_op jit(solution)/shard_map/ppermute | solution.py:156
  146.8 2.2 collective-permute-start.13
  149.0 2.6 %collective-permute-start.12 = (bf16[128,256]{1,0:T(8,128)(2,1)S(1)}, bf16[128,256]{1,0:T(8,128)(2,1)S(1)}, u32[]{:S(2)}, u32[]{:S(2)}) collective-permute-start(bf16[128,256]{1,0:T(8,128)(2,1)S(1)} %copy-done.27), channel_id=1, source_target_pairs={{0,13},{1,14},{2,15},{3,0},{4,1},{5,2},{6,3},{7,4},{8,5},{9,6},{10... | collective-permute-start | bytes 196616 | tf_op jit(solution)/shard_map/ppermute | solution.py:156
  151.6 5.0 %collective-permute-start.11 = (bf16[128,256]{1,0:T(8,128)(2,1)S(1)}, bf16[128,256]{1,0:T(8,128)(2,1)S(1)}, u32[]{:S(2)}, u32[]{:S(2)}) collective-permute-start(bf16[128,256]{1,0:T(8,128)(2,1)S(1)} %copy-done.25), channel_id=1, source_target_pairs={{0,12},{1,13},{2,14},{3,15},{4,0},{5,1},{6,2},{7,3},{8,4},{9,5},{1... | collective-permute-start | bytes 196616 | tf_op jit(solution)/shard_map/ppermute | solution.py:156
  156.6 5.3 %collective-permute-start.10 = (bf16[128,256]{1,0:T(8,128)(2,1)S(1)}, bf16[128,256]{1,0:T(8,128)(2,1)S(1)}, u32[]{:S(2)}, u32[]{:S(2)}) collective-permute-start(bf16[128,256]{1,0:T(8,128)(2,1)S(1)} %copy-done.23), channel_id=1, source_target_pairs={{0,11},{1,12},{2,13},{3,14},{4,15},{5,0},{6,1},{7,2},{8,3},{9,4},{... | collective-permute-start | bytes 196616 | tf_op jit(solution)/shard_map/ppermute | solution.py:156
  162.0 5.4 %collective-permute-start.9 = (bf16[128,256]{1,0:T(8,128)(2,1)S(1)}, bf16[128,256]{1,0:T(8,128)(2,1)S(1)}, u32[]{:S(2)}, u32[]{:S(2)}) collective-permute-start(bf16[128,256]{1,0:T(8,128)(2,1)S(1)} %copy-done.21), channel_id=1, source_target_pairs={{0,10},{1,11},{2,12},{3,13},{4,14},{5,15},{6,0},{7,1},{8,2},{9,3},... | collective-permute-start | bytes 196616 | tf_op jit(solution)/shard_map/ppermute | solution.py:156
  167.4 6.5 %collective-permute-start.8 = (bf16[128,256]{1,0:T(8,128)(2,1)S(1)}, bf16[128,256]{1,0:T(8,128)(2,1)S(1)}, u32[]{:S(2)}, u32[]{:S(2)}) collective-permute-start(bf16[128,256]{1,0:T(8,128)(2,1)S(1)} %copy-done.19), channel_id=1, source_target_pairs={{0,9},{1,10},{2,11},{3,12},{4,13},{5,14},{6,15},{7,0},{8,1},{9,2},... | collective-permute-start | bytes 196616 | tf_op jit(solution)/shard_map/ppermute | solution.py:156
  173.9 7.4 %collective-permute-start.7 = (bf16[128,256]{1,0:T(8,128)(2,1)S(1)}, bf16[128,256]{1,0:T(8,128)(2,1)S(1)}, u32[]{:S(2)}, u32[]{:S(2)}) collective-permute-start(bf16[128,256]{1,0:T(8,128)(2,1)S(1)} %copy-done.17), channel_id=1, source_target_pairs={{0,8},{1,9},{2,10},{3,11},{4,12},{5,13},{6,14},{7,15},{8,0},{9,1},... | collective-permute-start | bytes 196616 | tf_op jit(solution)/shard_map/ppermute | solution.py:156
  181.3 6.5 %collective-permute-start.6 = (bf16[128,256]{1,0:T(8,128)(2,1)S(1)}, bf16[128,256]{1,0:T(8,128)(2,1)S(1)}, u32[]{:S(2)}, u32[]{:S(2)}) collective-permute-start(bf16[128,256]{1,0:T(8,128)(2,1)S(1)} %copy-done.15), channel_id=1, source_target_pairs={{0,7},{1,8},{2,9},{3,10},{4,11},{5,12},{6,13},{7,14},{8,15},{9,0},... | collective-permute-start | bytes 196616 | tf_op jit(solution)/shard_map/ppermute | solution.py:156
  187.8 4.2 %collective-permute-start.5 = (bf16[128,256]{1,0:T(8,128)(2,1)S(1)}, bf16[128,256]{1,0:T(8,128)(2,1)S(1)}, u32[]{:S(2)}, u32[]{:S(2)}) collective-permute-start(bf16[128,256]{1,0:T(8,128)(2,1)S(1)} %copy-done.13), channel_id=1, source_target_pairs={{0,6},{1,7},{2,8},{3,9},{4,10},{5,11},{6,12},{7,13},{8,14},{9,15},... | collective-permute-start | bytes 196616 | tf_op jit(solution)/shard_map/ppermute | solution.py:156
  192.0 7.3 %collective-permute-start.4 = (bf16[128,256]{1,0:T(8,128)(2,1)S(1)}, bf16[128,256]{1,0:T(8,128)(2,1)S(1)}, u32[]{:S(2)}, u32[]{:S(2)}) collective-permute-start(bf16[128,256]{1,0:T(8,128)(2,1)S(1)} %copy-done.11), channel_id=1, source_target_pairs={{0,5},{1,6},{2,7},{3,8},{4,9},{5,10},{6,11},{7,12},{8,13},{9,14},{... | collective-permute-start | bytes 196616 | tf_op jit(solution)/shard_map/ppermute | solution.py:156
  199.4 3.9 %collective-permute-start.3 = (bf16[128,256]{1,0:T(8,128)(2,1)S(1)}, bf16[128,256]{1,0:T(8,128)(2,1)S(1)}, u32[]{:S(2)}, u32[]{:S(2)}) collective-permute-start(bf16[128,256]{1,0:T(8,128)(2,1)S(1)} %copy-done.9), channel_id=1, source_target_pairs={{0,4},{1,5},{2,6},{3,7},{4,8},{5,9},{6,10},{7,11},{8,12},{9,13},{1... | collective-permute-start | bytes 196616 | tf_op jit(solution)/shard_map/ppermute | solution.py:156
  203.3 3.8 %collective-permute-start.2 = (bf16[128,256]{1,0:T(8,128)(2,1)S(1)}, bf16[128,256]{1,0:T(8,128)(2,1)S(1)}, u32[]{:S(2)}, u32[]{:S(2)}) collective-permute-start(bf16[128,256]{1,0:T(8,128)(2,1)S(1)} %copy-done.7), channel_id=1, source_target_pairs={{0,3},{1,4},{2,5},{3,6},{4,7},{5,8},{6,9},{7,10},{8,11},{9,12},{10... | collective-permute-start | bytes 196616 | tf_op jit(solution)/shard_map/ppermute | solution.py:156
  207.1 2.6 %collective-permute-start.1 = (bf16[128,256]{1,0:T(8,128)(2,1)S(1)}, bf16[128,256]{1,0:T(8,128)(2,1)S(1)}, u32[]{:S(2)}, u32[]{:S(2)}) collective-permute-start(bf16[128,256]{1,0:T(8,128)(2,1)S(1)} %copy-done.5), channel_id=1, source_target_pairs={{0,2},{1,3},{2,4},{3,5},{4,6},{5,7},{6,8},{7,9},{8,10},{9,11},{10,... | collective-permute-start | bytes 196616 | tf_op jit(solution)/shard_map/ppermute | solution.py:156
  210.1 3.9 %collective-permute-start = (bf16[128,256]{1,0:T(8,128)(2,1)S(1)}, bf16[128,256]{1,0:T(8,128)(2,1)S(1)}, u32[]{:S(2)}, u32[]{:S(2)}) collective-permute-start(bf16[128,256]{1,0:T(8,128)(2,1)S(1)} %copy-done.3), channel_id=1, source_target_pairs={{0,1},{1,2},{2,3},{3,4},{4,5},{5,6},{6,7},{7,8},{8,9},{9,10},{10,1... | collective-permute-start | bytes 196616 | tf_op jit(solution)/shard_map/ppermute | solution.py:156
  214.0 4.5 %collective-permute-done.4 = bf16[128,256]{1,0:T(8,128)(2,1)S(1)} collective-permute-done((bf16[128,256]{1,0:T(8,128)(2,1)S(1)}, bf16[128,256]{1,0:T(8,128)(2,1)S(1)}, u32[]{:S(2)}, u32[]{:S(2)}) %collective-permute-start.4) | collective-permute-done | bytes 65568 | tf_op jit(solution)/shard_map/ppermute | solution.py:156
  218.6 6.2 %collective-permute-done.3 = bf16[128,256]{1,0:T(8,128)(2,1)S(1)} collective-permute-done((bf16[128,256]{1,0:T(8,128)(2,1)S(1)}, bf16[128,256]{1,0:T(8,128)(2,1)S(1)}, u32[]{:S(2)}, u32[]{:S(2)}) %collective-permute-start.3) | collective-permute-done | bytes 65568 | tf_op jit(solution)/shard_map/ppermute | solution.py:156
  224.7 4.3 %collective-permute-done.1 = bf16[128,256]{1,0:T(8,128)(2,1)S(1)} collective-permute-done((bf16[128,256]{1,0:T(8,128)(2,1)S(1)}, bf16[128,256]{1,0:T(8,128)(2,1)S(1)}, u32[]{:S(2)}, u32[]{:S(2)}) %collective-permute-start.1) | collective-permute-done | bytes 65568 | tf_op jit(solution)/shard_map/ppermute | solution.py:156
  229.1 1.1 collective-permute-done
  230.2 0.8 convert_add_fusion
  231.0 1.1 bitcast_convert_fusion
  (82 shorter events, 3.0 us)
Async XLA Ops:
  7.2 1.0 copy-start
  7.2 14.2 %copy-start.32 = (s32[16,64]{1,0:T(8,128)S(1)}, s32[16,64]{1,0:T(8,128)}, u32[]{:S(2)}) copy-start(s32[16,64]{1,0:T(8,128)} %param.7) | copy-start | bytes 12292
  7.2 14.6 %copy-start.33 = (s32[2048]{0:T(1024)S(1)}, s32[2048]{0:T(1024)}, u32[]{:S(2)}) copy-start(s32[2048]{0:T(1024)} %param.8) | copy-start | bytes 24580
  7.2 28.5 %copy-start.1 = (bf16[2048,256]{1,0:T(8,128)(2,1)S(1)}, bf16[2048,256]{1,0:T(8,128)(2,1)}, u32[]{:S(2)}) copy-start(bf16[2048,256]{1,0:T(8,128)(2,1)} %user_ref.3) | copy-start | bytes 3145732
  7.2 80.2 %all-gather.2.cloned.1.call-start = ((), (), s32[]{:S(2)}) async-start(), calls=%async_computation.5 | async-start | bytes 2162688 | tf_op jit(solution)/shard_map/all_gather | solution.py:107
  10.9 24.8 %all-to-all-start = ((bf16[32,32,384]{2,1,0:T(8,128)(2,1)}), bf16[32,32,384]{2,1,0:T(8,128)(2,1)S(1)}, u32[]{:S(2)}, u32[]{:S(2)}) async-start(bf16[32,32,384]{2,1,0:T(8,128)(2,1)} %broadcast_in_dim.21), calls=%async_computation | async-start | bytes 1572864 | tf_op jit(solution)/shard_map/all_to_all | solution.py:19
  79.3 0.6 copy-start.6
  79.9 0.6 copy-start.8
  80.5 0.6 copy-start.10
  81.2 0.6 copy-start.12
  81.8 0.6 copy-start.14
  82.4 0.6 copy-start.16
  83.0 0.6 copy-start.18
  83.7 0.6 copy-start.20
  84.3 0.6 copy-start.22
  85.6 0.6 copy-start.26
  86.8 0.6 copy-start.30
  90.6 50.3 %copy-start.31 = (bf16[128,256]{1,0:T(8,128)(2,1)S(1)}, bf16[128,256]{1,0:T(8,128)(2,1)}, u32[]{:S(2)}) copy-start(bf16[128,256]{1,0:T(8,128)(2,1)} %copy-done.30) | copy-start | bytes 196612
  90.7 56.2 %copy-start.29 = (bf16[128,256]{1,0:T(8,128)(2,1)S(1)}, bf16[128,256]{1,0:T(8,128)(2,1)}, u32[]{:S(2)}) copy-start(bf16[128,256]{1,0:T(8,128)(2,1)} %copy-done.28) | copy-start | bytes 196612
  90.7 58.4 %copy-start.27 = (bf16[128,256]{1,0:T(8,128)(2,1)S(1)}, bf16[128,256]{1,0:T(8,128)(2,1)}, u32[]{:S(2)}) copy-start(bf16[128,256]{1,0:T(8,128)(2,1)} %copy-done.26) | copy-start | bytes 196612
  90.7 61.0 %copy-start.25 = (bf16[128,256]{1,0:T(8,128)(2,1)S(1)}, bf16[128,256]{1,0:T(8,128)(2,1)}, u32[]{:S(2)}) copy-start(bf16[128,256]{1,0:T(8,128)(2,1)} %copy-done.24) | copy-start | bytes 196612
  90.7 65.9 %copy-start.23 = (bf16[128,256]{1,0:T(8,128)(2,1)S(1)}, bf16[128,256]{1,0:T(8,128)(2,1)}, u32[]{:S(2)}) copy-start(bf16[128,256]{1,0:T(8,128)(2,1)} %copy-done.22) | copy-start | bytes 196612
  90.7 71.3 %copy-start.21 = (bf16[128,256]{1,0:T(8,128)(2,1)S(1)}, bf16[128,256]{1,0:T(8,128)(2,1)}, u32[]{:S(2)}) copy-start(bf16[128,256]{1,0:T(8,128)(2,1)} %copy-done.20) | copy-start | bytes 196612
  90.7 76.7 %copy-start.19 = (bf16[128,256]{1,0:T(8,128)(2,1)S(1)}, bf16[128,256]{1,0:T(8,128)(2,1)}, u32[]{:S(2)}) copy-start(bf16[128,256]{1,0:T(8,128)(2,1)} %copy-done.18) | copy-start | bytes 196612
  90.7 83.2 %copy-start.17 = (bf16[128,256]{1,0:T(8,128)(2,1)S(1)}, bf16[128,256]{1,0:T(8,128)(2,1)}, u32[]{:S(2)}) copy-start(bf16[128,256]{1,0:T(8,128)(2,1)} %copy-done.16) | copy-start | bytes 196612
  90.7 90.6 %copy-start.15 = (bf16[128,256]{1,0:T(8,128)(2,1)S(1)}, bf16[128,256]{1,0:T(8,128)(2,1)}, u32[]{:S(2)}) copy-start(bf16[128,256]{1,0:T(8,128)(2,1)} %copy-done.14) | copy-start | bytes 196612
  90.7 97.1 %copy-start.13 = (bf16[128,256]{1,0:T(8,128)(2,1)S(1)}, bf16[128,256]{1,0:T(8,128)(2,1)}, u32[]{:S(2)}) copy-start(bf16[128,256]{1,0:T(8,128)(2,1)} %copy-done.12) | copy-start | bytes 196612
  90.7 101.3 %copy-start.11 = (bf16[128,256]{1,0:T(8,128)(2,1)S(1)}, bf16[128,256]{1,0:T(8,128)(2,1)}, u32[]{:S(2)}) copy-start(bf16[128,256]{1,0:T(8,128)(2,1)} %copy-done.10) | copy-start | bytes 196612
  90.8 108.6 %copy-start.9 = (bf16[128,256]{1,0:T(8,128)(2,1)S(1)}, bf16[128,256]{1,0:T(8,128)(2,1)}, u32[]{:S(2)}) copy-start(bf16[128,256]{1,0:T(8,128)(2,1)} %copy-done.8) | copy-start | bytes 196612
  90.8 112.5 %copy-start.7 = (bf16[128,256]{1,0:T(8,128)(2,1)S(1)}, bf16[128,256]{1,0:T(8,128)(2,1)}, u32[]{:S(2)}) copy-start(bf16[128,256]{1,0:T(8,128)(2,1)} %copy-done.6) | copy-start | bytes 196612
  90.8 116.3 %copy-start.5 = (bf16[128,256]{1,0:T(8,128)(2,1)S(1)}, bf16[128,256]{1,0:T(8,128)(2,1)}, u32[]{:S(2)}) copy-start(bf16[128,256]{1,0:T(8,128)(2,1)} %copy-done.4) | copy-start | bytes 196612
  90.8 119.3 %copy-start.3 = (bf16[128,256]{1,0:T(8,128)(2,1)S(1)}, bf16[128,256]{1,0:T(8,128)(2,1)}, u32[]{:S(2)}) copy-start(bf16[128,256]{1,0:T(8,128)(2,1)} %copy-done.2) | copy-start | bytes 196612
  132.0 99.0 %all-to-all-start.4 = ((bf16[32,32,256]{2,1,0:T(8,128)(2,1)}), bf16[32,32,256]{2,1,0:T(8,128)(2,1)S(1)}, u32[]{:S(2)}, u32[]{:S(2)}) async-start(bf16[32,32,256]{2,1,0:T(8,128)(2,1)} %broadcast_in_dim.50), calls=%async_computation.4 | async-start | bytes 1048576 | tf_op jit(solution)/shard_map/all_to_all | solution.py:19
  141.0 21.0 %collective-permute-start.14 = (bf16[128,256]{1,0:T(8,128)(2,1)S(1)}, bf16[128,256]{1,0:T(8,128)(2,1)S(1)}, u32[]{:S(2)}, u32[]{:S(2)}) collective-permute-start(bf16[128,256]{1,0:T(8,128)(2,1)S(1)} %copy-done.31), channel_id=1, source_target_pairs={{0,15},{1,0},{2,1},{3,2},{4,3},{5,4},{6,5},{7,6},{8,7},{9,8},{10,9... | collective-permute-start | bytes 196616 | tf_op jit(solution)/shard_map/ppermute | solution.py:156
  146.8 20.6 %collective-permute-start.13 = (bf16[128,256]{1,0:T(8,128)(2,1)S(1)}, bf16[128,256]{1,0:T(8,128)(2,1)S(1)}, u32[]{:S(2)}, u32[]{:S(2)}) collective-permute-start(bf16[128,256]{1,0:T(8,128)(2,1)S(1)} %copy-done.29), channel_id=1, source_target_pairs={{0,14},{1,15},{2,0},{3,1},{4,2},{5,3},{6,4},{7,5},{8,6},{9,7},{10,... | collective-permute-start | bytes 196616 | tf_op jit(solution)/shard_map/ppermute | solution.py:156
  149.0 24.9 %collective-permute-start.12 = (bf16[128,256]{1,0:T(8,128)(2,1)S(1)}, bf16[128,256]{1,0:T(8,128)(2,1)S(1)}, u32[]{:S(2)}, u32[]{:S(2)}) collective-permute-start(bf16[128,256]{1,0:T(8,128)(2,1)S(1)} %copy-done.27), channel_id=1, source_target_pairs={{0,13},{1,14},{2,15},{3,0},{4,1},{5,2},{6,3},{7,4},{8,5},{9,6},{10... | collective-permute-start | bytes 196616 | tf_op jit(solution)/shard_map/ppermute | solution.py:156
  151.6 29.6 %collective-permute-start.11 = (bf16[128,256]{1,0:T(8,128)(2,1)S(1)}, bf16[128,256]{1,0:T(8,128)(2,1)S(1)}, u32[]{:S(2)}, u32[]{:S(2)}) collective-permute-start(bf16[128,256]{1,0:T(8,128)(2,1)S(1)} %copy-done.25), channel_id=1, source_target_pairs={{0,12},{1,13},{2,14},{3,15},{4,0},{5,1},{6,2},{7,3},{8,4},{9,5},{1... | collective-permute-start | bytes 196616 | tf_op jit(solution)/shard_map/ppermute | solution.py:156
  156.6 31.2 %collective-permute-start.10 = (bf16[128,256]{1,0:T(8,128)(2,1)S(1)}, bf16[128,256]{1,0:T(8,128)(2,1)S(1)}, u32[]{:S(2)}, u32[]{:S(2)}) collective-permute-start(bf16[128,256]{1,0:T(8,128)(2,1)S(1)} %copy-done.23), channel_id=1, source_target_pairs={{0,11},{1,12},{2,13},{3,14},{4,15},{5,0},{6,1},{7,2},{8,3},{9,4},{... | collective-permute-start | bytes 196616 | tf_op jit(solution)/shard_map/ppermute | solution.py:156
  162.0 30.0 %collective-permute-start.9 = (bf16[128,256]{1,0:T(8,128)(2,1)S(1)}, bf16[128,256]{1,0:T(8,128)(2,1)S(1)}, u32[]{:S(2)}, u32[]{:S(2)}) collective-permute-start(bf16[128,256]{1,0:T(8,128)(2,1)S(1)} %copy-done.21), channel_id=1, source_target_pairs={{0,10},{1,11},{2,12},{3,13},{4,14},{5,15},{6,0},{7,1},{8,2},{9,3},... | collective-permute-start | bytes 196616 | tf_op jit(solution)/shard_map/ppermute | solution.py:156
  167.4 31.9 %collective-permute-start.8 = (bf16[128,256]{1,0:T(8,128)(2,1)S(1)}, bf16[128,256]{1,0:T(8,128)(2,1)S(1)}, u32[]{:S(2)}, u32[]{:S(2)}) collective-permute-start(bf16[128,256]{1,0:T(8,128)(2,1)S(1)} %copy-done.19), channel_id=1, source_target_pairs={{0,9},{1,10},{2,11},{3,12},{4,13},{5,14},{6,15},{7,0},{8,1},{9,2},... | collective-permute-start | bytes 196616 | tf_op jit(solution)/shard_map/ppermute | solution.py:156
  173.9 29.4 %collective-permute-start.7 = (bf16[128,256]{1,0:T(8,128)(2,1)S(1)}, bf16[128,256]{1,0:T(8,128)(2,1)S(1)}, u32[]{:S(2)}, u32[]{:S(2)}) collective-permute-start(bf16[128,256]{1,0:T(8,128)(2,1)S(1)} %copy-done.17), channel_id=1, source_target_pairs={{0,8},{1,9},{2,10},{3,11},{4,12},{5,13},{6,14},{7,15},{8,0},{9,1},... | collective-permute-start | bytes 196616 | tf_op jit(solution)/shard_map/ppermute | solution.py:156
  181.3 25.8 %collective-permute-start.6 = (bf16[128,256]{1,0:T(8,128)(2,1)S(1)}, bf16[128,256]{1,0:T(8,128)(2,1)S(1)}, u32[]{:S(2)}, u32[]{:S(2)}) collective-permute-start(bf16[128,256]{1,0:T(8,128)(2,1)S(1)} %copy-done.15), channel_id=1, source_target_pairs={{0,7},{1,8},{2,9},{3,10},{4,11},{5,12},{6,13},{7,14},{8,15},{9,0},... | collective-permute-start | bytes 196616 | tf_op jit(solution)/shard_map/ppermute | solution.py:156
  187.8 22.3 %collective-permute-start.5 = (bf16[128,256]{1,0:T(8,128)(2,1)S(1)}, bf16[128,256]{1,0:T(8,128)(2,1)S(1)}, u32[]{:S(2)}, u32[]{:S(2)}) collective-permute-start(bf16[128,256]{1,0:T(8,128)(2,1)S(1)} %copy-done.13), channel_id=1, source_target_pairs={{0,6},{1,7},{2,8},{3,9},{4,10},{5,11},{6,12},{7,13},{8,14},{9,15},... | collective-permute-start | bytes 196616 | tf_op jit(solution)/shard_map/ppermute | solution.py:156
  192.0 26.5 %collective-permute-start.4 = (bf16[128,256]{1,0:T(8,128)(2,1)S(1)}, bf16[128,256]{1,0:T(8,128)(2,1)S(1)}, u32[]{:S(2)}, u32[]{:S(2)}) collective-permute-start(bf16[128,256]{1,0:T(8,128)(2,1)S(1)} %copy-done.11), channel_id=1, source_target_pairs={{0,5},{1,6},{2,7},{3,8},{4,9},{5,10},{6,11},{7,12},{8,13},{9,14},{... | collective-permute-start | bytes 196616 | tf_op jit(solution)/shard_map/ppermute | solution.py:156
  199.4 25.4 %collective-permute-start.3 = (bf16[128,256]{1,0:T(8,128)(2,1)S(1)}, bf16[128,256]{1,0:T(8,128)(2,1)S(1)}, u32[]{:S(2)}, u32[]{:S(2)}) collective-permute-start(bf16[128,256]{1,0:T(8,128)(2,1)S(1)} %copy-done.9), channel_id=1, source_target_pairs={{0,4},{1,5},{2,6},{3,7},{4,8},{5,9},{6,10},{7,11},{8,12},{9,13},{1... | collective-permute-start | bytes 196616 | tf_op jit(solution)/shard_map/ppermute | solution.py:156
  203.3 21.4 %collective-permute-start.2 = (bf16[128,256]{1,0:T(8,128)(2,1)S(1)}, bf16[128,256]{1,0:T(8,128)(2,1)S(1)}, u32[]{:S(2)}, u32[]{:S(2)}) collective-permute-start(bf16[128,256]{1,0:T(8,128)(2,1)S(1)} %copy-done.7), channel_id=1, source_target_pairs={{0,3},{1,4},{2,5},{3,6},{4,7},{5,8},{6,9},{7,10},{8,11},{9,12},{10... | collective-permute-start | bytes 196616 | tf_op jit(solution)/shard_map/ppermute | solution.py:156
  207.1 21.9 %collective-permute-start.1 = (bf16[128,256]{1,0:T(8,128)(2,1)S(1)}, bf16[128,256]{1,0:T(8,128)(2,1)S(1)}, u32[]{:S(2)}, u32[]{:S(2)}) collective-permute-start(bf16[128,256]{1,0:T(8,128)(2,1)S(1)} %copy-done.5), channel_id=1, source_target_pairs={{0,2},{1,3},{2,4},{3,5},{4,6},{5,7},{6,8},{7,9},{8,10},{9,11},{10,... | collective-permute-start | bytes 196616 | tf_op jit(solution)/shard_map/ppermute | solution.py:156
  210.1 20.1 %collective-permute-start = (bf16[128,256]{1,0:T(8,128)(2,1)S(1)}, bf16[128,256]{1,0:T(8,128)(2,1)S(1)}, u32[]{:S(2)}, u32[]{:S(2)}) collective-permute-start(bf16[128,256]{1,0:T(8,128)(2,1)S(1)} %copy-done.3), channel_id=1, source_target_pairs={{0,1},{1,2},{2,3},{3,4},{4,5},{5,6},{6,7},{7,8},{8,9},{9,10},{10,1... | collective-permute-start | bytes 196616 | tf_op jit(solution)/shard_map/ppermute | solution.py:156
  (4 other events, 2.5 us)
Sparse Core Ops, SparseCore 0:
  11.2 64.8 all-gather.1

commit v3 on v1

--- a/solution.py
+++ b/solution.py
@@ -74,7 +74,7 @@
     soft = soft + jnp.where(at_positive(raw, pos_ref), row_of(weight_ref), 0.0)
     soft = soft.astype(bf16)
     sums[...] += jnp.dot(soft, user_ref[...], preferred_element_type=f32)
-    grad_ref[...] = jnp.dot(item_t[...], soft, preferred_element_type=f32).T.astype(bf16)
+    grad_ref[...] = jnp.dot(item_t[...], soft, preferred_element_type=f32).T
 
     @pl.when(step == pl.num_programs(0) - 1)
     def _():
@@ -128,7 +128,7 @@
             pl.BlockSpec((blocks, BU), lambda i: (0, 0)),
         ],
         out_shape=[
-            jax.ShapeDtypeStruct((users, width), bf16),
+            jax.ShapeDtypeStruct((users, width), f32),
             jax.ShapeDtypeStruct((rows, 2 * width), bf16),
             jax.ShapeDtypeStruct((blocks, BU), f32),
         ],
@@ -141,6 +141,8 @@
         compiler_params=params,
     )(items, user_emb, mask, pos_row, stats)
 
+    user_grad = lax.psum_scatter(grad, "items", scatter_dimension=0, tiled=True)
+
     part = lax.dot_general(feats, high, (((0,), (0,)), ((), ())), preferred_element_type=f32)
     part = (part[:, :width] + part[:, width:]).astype(bf16)
     cut = part.shape[0] // group
@@ -149,8 +151,6 @@
     part = jnp.sum(spread(part, "items", shards).astype(f32), axis=0).astype(bf16)
     weight_grad = spread(part, "users", group).reshape(group * cut, width).astype(f32)
 
-    grad = lax.all_to_all(grad.reshape(shards, users // shards, width), "items", 0, 0)
-    user_grad = jnp.sum(grad.astype(f32), axis=0)
     return loss.reshape(users), user_grad, weight_grad
 
 

time: 207 us -> 165 us (0.80)
  the two profiles are of different devices: /device:TPU:1 before, /device:TPU:2 now
where the time goes in v3:
time: 165 us; the launch traced here: 164 us
  blocking collectives  89.8 us (54%)
  waiting for transfers between devices  25.4 us (15%)
  between operations  15.6 us (9%)
  Pallas kernels  14.7 us (9%)
  starting transfers between devices  9.56 us (6%)
  matrix products  3.88 us (2%)
  local copies, waits for them, and re-layouts  3.73 us (2%)
    all_to_all x3, blocking collectives, spread(): return lax.all_to_all(jnp.broadcast_to(x[None], (n,) + x.shape), axis, 0, 0)  74.7 us
    all_to_all x1, blocking collectives, body(): part = lax.all_to_all(part.reshape(group, cut, width), 'users', 0, 0)  15.1 us
    all_to_all x1, waiting for transfers between devices, spread(): return lax.all_to_all(jnp.broadcast_to(x[None], (n,) + x.shape), axis, 0, 0)  12.9 us
    reduce_scatter x1, waiting for transfers between devices, body(): user_grad = lax.psum_scatter(grad, 'items', scatter_dimension=0, tiled=True)  11.8 us
    all_to_all x1, starting transfers between devices, spread(): return lax.all_to_all(jnp.broadcast_to(x[None], (n,) + x.shape), axis, 0, 0)  9.48 us
    pallas_call x1, Pallas kernels, body(): pl.pallas_call(backward, grid=(steps,), in_specs=in_specs + [pl.BlockSpec...  9.26 us
    pallas_call x1, Pallas kernels, body(): pl.pallas_call(forward, grid=(steps,), in_specs=in_specs, out_specs=pl.Bl...  5.44 us
  transfers between devices with their start and end apart: 3, of which 2 were waited for; matrix products, arithmetic and copies ran while one was open for 5% of the time, Pallas kernels for 9%

profile of v3, /device:TPU:2, one launch (start us, length us, event | category | flops | bytes accessed | tf_op | source)
XLA Modules:
  0.0 164.3 jit_solution(3953207509776376603)
XLA Ops:
  8.0 0.0 copy-start
  8.0 0.0 copy-start.3
  8.0 0.0 copy-start.4
  8.0 0.0 copy-start.1
  8.0 0.0 all-gather.2.cloned.1.call-start
  8.1 0.7 all-gather.2.cloned.1.call-update
  8.8 0.3 copy-done
  9.0 1.0 convolution_convert_fusion
  10.1 0.7 broadcast_in_dim.20
  10.8 1.0 broadcast_in_dim.21
  11.8 9.5 %all-to-all-start = ((bf16[32,32,384]{2,1,0:T(8,128)(2,1)}), bf16[32,32,384]{2,1,0:T(8,128)(2,1)S(1)}, u32[]{:S(2)}, u32[]{:S(2)}) async-start(bf16[32,32,384]{2,1,0:T(8,128)(2,1)} %broadcast_in_dim.21), calls=%async_computation | async-start | bytes 1572864 | tf_op jit(solution)/shard_map/all_to_all | solution.py:19
  21.3 0.0 reduce-scatter.2.cloned.1.call-start
  21.3 0.0 copy-done.3
  21.3 0.3 compare_reduce_fusion
  21.6 0.1 copy.10
  21.7 0.0 copy-done.4
  21.7 0.1 broadcast_bitcast_fusion.mask_ref
  21.8 12.9 %all-to-all-done = bf16[32,32,384]{2,1,0:T(8,128)(2,1)S(1)} async-done(((bf16[32,32,384]{2,1,0:T(8,128)(2,1)}), bf16[32,32,384]{2,1,0:T(8,128)(2,1)S(1)}, u32[]{:S(2)}, u32[]{:S(2)}) %all-to-all-start) | async-done | bytes 786464 | tf_op jit(solution)/shard_map/all_to_all | solution.py:19
  34.7 0.0 copy-done.1
  34.7 5.4 %shard_map.85 = f32[32,128]{1,0:T(8,128)S(1)} custom-call(bf16[1024,384]{1,0:T(8,128)(2,1)S(1)} %bitcast.15, bf16[2048,256]{1,0:T(8,128)(2,1)S(1)} %copy-done.1, f32[8,2048]{1,0:T(8,128)S(1)} %broadcast_bitcast_fusion.mask_ref, s32[1,2048]{1,0:T(1,128)S(1)} %bitcast.17), custom_call_target="tpu_custom_call" | custom-call | tf_op jit(solution)/shard_map/pallas_call | solution.py:112
  40.1 31.7 %all_to_all.25.stat_ref = f32[16,32,128]{2,1,0:T(8,128)S(1)} all-to-all(f32[16,32,128]{2,1,0:T(8,128)S(1)} %broadcast_in_dim.25), channel_id=1, replica_groups=mesh['users'=32,'items'=16] {'items'}, dimensions={0} | all-to-all | bytes 524288 | tf_op jit(solution)/shard_map/all_to_all | solution.py:19
  71.9 9.3 %shard_map.86 = (f32[2048,256]{1,0:T(8,128)S(1)}, bf16[1024,512]{1,0:T(8,128)(2,1)S(1)}, f32[16,128]{1,0:T(8,128)}) custom-call(bf16[1024,384]{1,0:T(8,128)(2,1)S(1)} %bitcast.16, bf16[2048,256]{1,0:T(8,128)(2,1)S(1)} %copy-done.1, f32[8,2048]{1,0:T(8,128)S(1)} %broadcast_bitcast_fusion.mask_ref, s32[1,2048]{1,0:T(1,128)S(1)} %bitcast.18, ...), custom_call_target="tpu_custom_call" | custom-call | tf_op jit(solution)/shard_map/pallas_call | solution.py:121
  81.1 0.0 copy-start.2
  81.1 1.3 copy-done.2
  82.4 0.0 reduce-scatter.2.cloned.1.call-update
  82.4 0.0 all-gather.2.cloned.1.call-done
  82.5 2.9 %convolution_bitcast_fusion = f32[1024,512]{0,1:T(8,128)S(1)} fusion(bf16[1024,512]{1,0:T(8,128)(2,1)S(1)} %get-tuple-element.8, bf16[1024,1024]{1,0:T(8,128)(2,1)} %all-gather.2.cloned.1.call-done), kind=kOutput, calls=%fused_computation | convolution fusion | flops 1073741824 | bytes 5242880 | tf_op jit(solution)/shard_map/dot_general | solution.py:146
  85.3 0.1 fusion
  85.5 0.2 copy.11
  85.7 15.1 %all_to_all.26 = bf16[32,32,256]{2,1,0:T(8,128)(2,1)S(1)} all-to-all(bf16[32,32,256]{2,1,0:T(8,128)(2,1)S(1)} %bitcast.19), channel_id=1, replica_groups=mesh['users'=32,'items'=16] {'users'}, dimensions={0} | all-to-all | bytes 1048576 | tf_op jit(solution)/shard_map/all_to_all | solution.py:149
  100.8 0.1 reduce_sum.24
  100.9 26.9 %all_to_all.27 = bf16[16,32,256]{2,1,0:T(8,128)(2,1)S(1)} all-to-all(bf16[16,32,256]{2,1,0:T(8,128)(2,1)S(1)} %broadcast_in_dim.26), channel_id=1, replica_groups=mesh['users'=32,'items'=16] {'items'}, dimensions={0} | all-to-all | bytes 524288 | tf_op jit(solution)/shard_map/all_to_all | solution.py:19
  127.9 0.1 broadcast_in_dim.50
  127.9 16.0 %all_to_all.28 = bf16[32,32,256]{2,1,0:T(8,128)(2,1)S(1)} all-to-all(bf16[32,32,256]{2,1,0:T(8,128)(2,1)S(1)} %broadcast_in_dim.50), channel_id=1, replica_groups=mesh['users'=32,'items'=16] {'users'}, dimensions={0} | all-to-all | bytes 1048576 | tf_op jit(solution)/shard_map/all_to_all | solution.py:19
  144.0 1.1 bitcast_convert_fusion
  145.1 11.8 %reduce-scatter.2.cloned.1.call-done = f32[128,256]{1,0:T(8,128)} async-done(((f32[2048,256]{1,0:T(8,128)}), f32[128,256]{1,0:T(8,128)}) %reduce-scatter.2.cloned.1.call-update) | async-done | bytes 131088 | tf_op jit(solution)/shard_map/reduce_scatter | solution.py:144
  (7 shorter events, 0.1 us)
Async XLA Ops:
  8.0 1.0 copy-start
  8.0 13.3 %copy-start.3 = (s32[16,64]{1,0:T(8,128)S(1)}, s32[16,64]{1,0:T(8,128)}, u32[]{:S(2)}) copy-start(s32[16,64]{1,0:T(8,128)} %param.7) | copy-start | bytes 12292
  8.0 13.7 %copy-start.4 = (s32[2048]{0:T(1024)S(1)}, s32[2048]{0:T(1024)}, u32[]{:S(2)}) copy-start(s32[2048]{0:T(1024)} %param.8) | copy-start | bytes 24580
  8.0 26.6 %copy-start.1 = (bf16[2048,256]{1,0:T(8,128)(2,1)S(1)}, bf16[2048,256]{1,0:T(8,128)(2,1)}, u32[]{:S(2)}) copy-start(bf16[2048,256]{1,0:T(8,128)(2,1)} %user_ref.3) | copy-start | bytes 3145732
  8.0 74.4 %all-gather.2.cloned.1.call-start = ((), (), s32[]{:S(2)}) async-start(), calls=%async_computation.7 | async-start | bytes 2162688 | tf_op jit(solution)/shard_map/all_gather | solution.py:98
  11.8 22.9 %all-to-all-start = ((bf16[32,32,384]{2,1,0:T(8,128)(2,1)}), bf16[32,32,384]{2,1,0:T(8,128)(2,1)S(1)}, u32[]{:S(2)}, u32[]{:S(2)}) async-start(bf16[32,32,384]{2,1,0:T(8,128)(2,1)} %broadcast_in_dim.21), calls=%async_computation | async-start | bytes 1572864 | tf_op jit(solution)/shard_map/all_to_all | solution.py:19
  21.3 135.6 %reduce-scatter.2.cloned.1.call-start = ((), (), s32[]{:S(2)}) async-start(), calls=%async_computation.6 | async-start | bytes 2228224 | tf_op jit(solution)/shard_map/reduce_scatter | solution.py:144
  81.1 1.3 copy-start.2
Sparse Core Ops, SparseCore 0:
  12.0 63.1 all-gather.1
Sparse Core Ops, SparseCore 1:
  82.5 74.3 reduce-scatter.1

commit v4 on v3

--- a/solution.py
+++ b/solution.py
@@ -7,9 +7,10 @@
 
 CL = 128
 BU = 128
-STEP = 256
+STEP = 1024
 NEG = -1e30
 FLOOR = -1e29
+PIECES = 3
 NT = (((1,), (1,)), ((), ()))
 f32 = jnp.float32
 bf16 = jnp.bfloat16
@@ -32,7 +33,7 @@
     return lax.broadcasted_iota(jnp.int32, raw.shape, 0) == pos_ref[...]
 
 
-def forward(item_ref, user_ref, mask_ref, pos_ref, stat_ref):
+def forward(item_ref, user_ref, mask_ref, pos_ref, lse_ref, own_ref, split_ref):
     step = pl.program_id(0)
     raw, kept = logits_of(item_ref, user_ref, mask_ref)
     here = (pos_ref[...] >= 0) & (pos_ref[...] < raw.shape[0])
@@ -41,27 +42,31 @@
     peak = jnp.maximum(jnp.maximum(jnp.max(kept, axis=0, keepdims=True), pos), FLOOR)
     total = jnp.sum(jnp.exp(kept - peak), axis=0, keepdims=True) + jnp.exp(pos - peak)
     lse = jnp.where(total > 0.0, peak + jnp.log(jnp.maximum(total, 1e-37)), NEG)
-    blocks = stat_ref.shape[0] // 2
     for h in range(STEP // BU):
         row = step * (STEP // BU) + h
-        stat_ref[pl.ds(row, 1), :] = lse[:, h * BU : (h + 1) * BU]
-        stat_ref[pl.ds(blocks + row, 1), :] = pos[:, h * BU : (h + 1) * BU]
+        lse_ref[pl.ds(row, 1), :] = lse[:, h * BU : (h + 1) * BU]
+        own_ref[pl.ds(row, 1), :] = pos[:, h * BU : (h + 1) * BU]
+    rest = jnp.where(here, pos, 0.0)
+    width = split_ref.shape[1]
+    for k in range(PIECES):
+        piece = rest.astype(bf16).astype(f32)
+        rest = rest - piece
+        for h in range(STEP // width):
+            row = k * (split_ref.shape[0] // PIECES) + step * (STEP // width) + h
+            split_ref[pl.ds(row, 1), :] = piece[:, h * width : (h + 1) * width]
 
 
-def backward(item_ref, user_ref, mask_ref, pos_ref, stat_ref, grad_ref, high_ref, loss_ref, item_t, total_ref, weight_ref, sums):
+def backward(item_ref, user_ref, mask_ref, pos_ref, lses_ref, own_ref, grad_ref, high_ref, total_ref, item_t, weight_ref, sums):
     step = pl.program_id(0)
     width = user_ref.shape[1]
-    blocks = loss_ref.shape[0]
 
     @pl.when(step == 0)
     def _():
-        lse = stat_ref[:, :blocks, :]
+        lse = lses_ref[...]
         peak = jnp.max(lse, axis=0)
         total = peak + jnp.log(jnp.sum(jnp.exp(lse - peak[None]), axis=0))
-        pos = jnp.max(stat_ref[:, blocks:, :], axis=0)
         total_ref[...] = total
-        loss_ref[...] = total - pos
-        weight_ref[...] = jnp.exp(pos - total) - 1.0
+        weight_ref[...] = jnp.exp(own_ref[...] - total) - 1.0
         item_t[...] = item_ref[:, :width].astype(f32).T.astype(bf16)
         sums[...] = jnp.zeros_like(sums)
 
@@ -108,38 +113,43 @@
         pl.BlockSpec((clus, STEP), lambda i: (0, i)),
         pl.BlockSpec((1, STEP), lambda i: (0, i)),
     ]
-    params = pltpu.CompilerParams(vmem_limit_bytes=40 << 20)
-    stat = pl.pallas_call(
+    params = pltpu.CompilerParams(vmem_limit_bytes=48 << 20)
+    table = pl.BlockSpec((blocks, BU), lambda i: (0, 0))
+    pieces = PIECES * users // width
+    lse, own_pos, split = pl.pallas_call(
         forward,
         grid=(steps,),
         in_specs=in_specs,
-        out_specs=pl.BlockSpec((2 * blocks, BU), lambda i: (0, 0)),
-        out_shape=jax.ShapeDtypeStruct((2 * blocks, BU), f32),
+        out_specs=[table, table, pl.BlockSpec((pieces, width), lambda i: (0, 0))],
+        out_shape=[
+            jax.ShapeDtypeStruct((blocks, BU), f32),
+            jax.ShapeDtypeStruct((blocks, BU), f32),
+            jax.ShapeDtypeStruct((pieces, width), f32),
+        ],
         compiler_params=params,
     )(items, user_emb, mask, pos_row)
-    stats = spread(stat, "items", shards)
-    grad, high, loss = pl.pallas_call(
+    lses = spread(lse, "items", shards)
+    grad, high, total = pl.pallas_call(
         backward,
         grid=(steps,),
-        in_specs=in_specs + [pl.BlockSpec((shards, 2 * blocks, BU), lambda i: (0, 0, 0))],
+        in_specs=in_specs + [pl.BlockSpec((shards, blocks, BU), lambda i: (0, 0, 0)), table],
         out_specs=[
             pl.BlockSpec((STEP, width), lambda i: (i, 0)),
             pl.BlockSpec((rows, 2 * width), lambda i: (0, 0)),
-            pl.BlockSpec((blocks, BU), lambda i: (0, 0)),
+            table,
         ],
         out_shape=[
-            jax.ShapeDtypeStruct((users, width), f32),
+            pltpu.HBM((users, width), f32),
             jax.ShapeDtypeStruct((rows, 2 * width), bf16),
             jax.ShapeDtypeStruct((blocks, BU), f32),
         ],
         scratch_shapes=[
             pltpu.VMEM((width, rows), bf16),
             pltpu.VMEM((blocks, BU), f32),
-            pltpu.VMEM((blocks, BU), f32),
             pltpu.VMEM((rows, width), f32),
         ],
         compiler_params=params,
-    )(items, user_emb, mask, pos_row, stats)
+    )(items, user_emb, mask, pos_row, lses, own_pos)
 
     user_grad = lax.psum_scatter(grad, "items", scatter_dimension=0, tiled=True)
 
@@ -148,10 +158,12 @@
     cut = part.shape[0] // group
     part = lax.all_to_all(part.reshape(group, cut, width), "users", 0, 0)
     part = jnp.sum(part.astype(f32), axis=0).astype(bf16)
-    part = jnp.sum(spread(part, "items", shards).astype(f32), axis=0).astype(bf16)
-    weight_grad = spread(part, "users", group).reshape(group * cut, width).astype(f32)
-
-    return loss.reshape(users), user_grad, weight_grad
+    both = spread(jnp.concatenate([part, split.astype(bf16)], axis=0), "items", shards)
+    both = jnp.sum(both.astype(f32), axis=0)
+    weight_grad = spread(both[:cut].astype(bf16), "users", group).reshape(group * cut, width).astype(f32)
+    pos_logit = jnp.sum(both[cut:].reshape(PIECES, users), axis=0)
+    user_loss = total.reshape(users) - pos_logit
+    return user_loss, user_grad, weight_grad
 
 
 def solution(mesh):

time: 165 us -> 169 us (1.024)
  the two profiles are of different devices: /device:TPU:2 before, /device:TPU:1 now
where the time goes in v4:
time: 169 us; the launch traced here: 168 us
  blocking collectives  62.3 us (37%)
  waiting for transfers between devices  42.4 us (25%)
  starting transfers between devices  27.4 us (16%)
  between operations  15.6 us (9%)
  Pallas kernels  10.1 us (6%)
  local copies, waits for them, and re-layouts  4.05 us (2%)
  matrix products  3.88 us (2%)
  other arithmetic  2.31 us (1%)
    all_to_all x2, blocking collectives, spread(): return lax.all_to_all(jnp.broadcast_to(x[None], (n,) + x.shape), axis, 0, 0)  62.3 us
    all_to_all x2, waiting for transfers between devices, spread(): return lax.all_to_all(jnp.broadcast_to(x[None], (n,) + x.shape), axis, 0, 0)  24.7 us
    all_to_all x2, starting transfers between devices, spread(): return lax.all_to_all(jnp.broadcast_to(x[None], (n,) + x.shape), axis, 0, 0)  22.3 us
    all_to_all x1, waiting for transfers between devices, body(): part = lax.all_to_all(part.reshape(group, cut, width), 'users', 0, 0)  11.5 us
    pallas_call x1, Pallas kernels, body(): pl.pallas_call(backward, grid=(steps,), in_specs=in_specs + [pl.BlockSpec...  6.01 us
    all_gather x1, waiting for transfers between devices, body(): feats = lax.all_gather(item_feat, 'users', axis=0, tiled=True)  5.44 us
    all_to_all x1, starting transfers between devices, body(): part = lax.all_to_all(part.reshape(group, cut, width), 'users', 0, 0)  5.11 us
    pallas_call x1, Pallas kernels, body(): pl.pallas_call(forward, grid=(steps,), in_specs=in_specs, out_specs=[tabl...  4.1 us
  transfers between devices with their start and end apart: 5, of which 4 were waited for; matrix products, arithmetic and copies ran while one was open for 6% of the time, Pallas kernels for 6%

profile of v4, /device:TPU:1, one launch (start us, length us, event | category | flops | bytes accessed | tf_op | source)
XLA Modules:
  0.0 168.1 jit_solution(9384973668933161324)
XLA Ops:
  8.0 0.0 copy-start
  8.0 0.0 copy-start.2
  8.0 0.0 copy-start.3
  8.0 0.0 copy-start.1
  8.0 0.0 all-gather.2.cloned.1.call-start
  8.1 0.7 all-gather.2.cloned.1.call-update
  8.8 0.3 copy-done
  9.0 1.0 convolution_convert_fusion
  10.1 0.7 broadcast_in_dim.20
  10.8 1.0 broadcast_in_dim.21
  11.8 10.4 %all-to-all-start = ((bf16[32,32,384]{2,1,0:T(8,128)(2,1)}), bf16[32,32,384]{2,1,0:T(8,128)(2,1)S(1)}, u32[]{:S(2)}, u32[]{:S(2)}) async-start(bf16[32,32,384]{2,1,0:T(8,128)(2,1)} %broadcast_in_dim.21), calls=%async_computation | async-start | bytes 1572864 | tf_op jit(solution)/shard_map/all_to_all | solution.py:20
  22.2 0.0 reduce-scatter.2.cloned.1.call-start
  22.3 0.0 copy-done.2
  22.3 0.3 compare_reduce_fusion
  22.6 0.1 copy.10
  22.7 0.0 copy-done.3
  22.7 0.1 broadcast_bitcast_fusion.mask_ref
  22.8 13.8 %all-to-all-done = bf16[32,32,384]{2,1,0:T(8,128)(2,1)S(1)} async-done(((bf16[32,32,384]{2,1,0:T(8,128)(2,1)}), bf16[32,32,384]{2,1,0:T(8,128)(2,1)S(1)}, u32[]{:S(2)}, u32[]{:S(2)}) %all-to-all-start) | async-done | bytes 786464 | tf_op jit(solution)/shard_map/all_to_all | solution.py:20
  36.6 0.0 copy-done.1
  36.6 4.1 %shard_map.85 = (f32[16,128]{1,0:T(8,128)S(1)}, f32[16,128]{1,0:T(8,128)S(1)}, f32[24,256]{1,0:T(8,128)S(1)}) custom-call(bf16[1024,384]{1,0:T(8,128)(2,1)S(1)} %bitcast.16, bf16[2048,256]{1,0:T(8,128)(2,1)S(1)} %copy-done.1, f32[8,2048]{1,0:T(8,128)S(1)} %broadcast_bitcast_fusion.mask_ref, s32[1,2048]{1,0:T(1,128)S(1)} %bitcast.18), custom_call_target="tpu_custom_call" | custom-call | tf_op jit(solution)/shard_map/pallas_call | solution.py:119
  40.7 24.8 %all_to_all.25.lses_ref = f32[16,16,128]{2,1,0:T(8,128)S(1)} all-to-all(f32[16,16,128]{2,1,0:T(8,128)S(1)} %broadcast_in_dim.25), channel_id=1, replica_groups=mesh['users'=32,'items'=16] {'items'}, dimensions={0} | all-to-all | bytes 262144 | tf_op jit(solution)/shard_map/all_to_all | solution.py:20
  65.4 6.0 %shard_map.86 = (f32[2048,256]{1,0:T(8,128)}, bf16[1024,512]{1,0:T(8,128)(2,1)S(1)}, f32[16,128]{1,0:T(8,128)S(1)}) custom-call(bf16[1024,384]{1,0:T(8,128)(2,1)S(1)} %bitcast.17, bf16[2048,256]{1,0:T(8,128)(2,1)S(1)} %copy-done.1, f32[8,2048]{1,0:T(8,128)S(1)} %broadcast_bitcast_fusion.mask_ref, s32[1,2048]{1,0:T(1,128)S(1)} %bitcast.19, ...), custom_call_target="tpu_custom_call" | custom-call | tf_op jit(solution)/shard_map/pallas_call | solution.py:132
  71.4 0.0 reduce-scatter.2.cloned.1.call-update
  71.5 5.4 %all-gather.2.cloned.1.call-done = bf16[1024,1024]{1,0:T(8,128)(2,1)} async-done(((bf16[32,1024]{1,0:T(8,128)(2,1)}), bf16[1024,1024]{1,0:T(8,128)(2,1)}) %all-gather.2.cloned.1.call-update) | async-done | bytes 2097168 | tf_op jit(solution)/shard_map/all_gather | solution.py:103
  76.9 2.9 %convolution_bitcast_fusion = f32[1024,512]{0,1:T(8,128)S(1)} fusion(bf16[1024,512]{1,0:T(8,128)(2,1)S(1)} %get-tuple-element.12, bf16[1024,1024]{1,0:T(8,128)(2,1)} %all-gather.2.cloned.1.call-done), kind=kOutput, calls=%fused_computation | convolution fusion | flops 1073741824 | bytes 5242880 | tf_op jit(solution)/shard_map/dot_general | solution.py:156
  79.8 0.1 fusion
  79.9 1.0 copy.11
  80.9 5.1 %all-to-all-start.2 = ((bf16[32,32,256]{2,1,0:T(8,128)(2,1)}), bf16[32,32,256]{2,1,0:T(8,128)(2,1)S(1)}, u32[]{:S(2)}, u32[]{:S(2)}) async-start(bf16[32,32,256]{2,1,0:T(8,128)(2,1)} %bitcast.5), calls=%async_computation.2 | async-start | bytes 1048576 | tf_op jit(solution)/shard_map/all_to_all | solution.py:159
  86.0 11.5 %all-to-all-done.2 = bf16[32,32,256]{2,1,0:T(8,128)(2,1)S(1)} async-done(((bf16[32,32,256]{2,1,0:T(8,128)(2,1)}), bf16[32,32,256]{2,1,0:T(8,128)(2,1)S(1)}, u32[]{:S(2)}, u32[]{:S(2)}) %all-to-all-start.2) | async-done | bytes 524320 | tf_op jit(solution)/shard_map/all_to_all | solution.py:159
  97.6 0.1 reduce_sum.30
  97.7 37.5 %all_to_all.26 = bf16[16,56,256]{2,1,0:T(8,128)(2,1)S(1)} all-to-all(bf16[16,56,256]{2,1,0:T(8,128)(2,1)S(1)} %broadcast_in_dim.26), channel_id=1, replica_groups=mesh['users'=32,'items'=16] {'items'}, dimensions={0} | all-to-all | bytes 917504 | tf_op jit(solution)/shard_map/all_to_all | solution.py:20
  135.2 0.1 convert_reduce_fusion
  135.3 0.9 broadcast_in_dim.50
  136.2 11.8 %all-to-all-start.4 = ((bf16[32,32,256]{2,1,0:T(8,128)(2,1)}), bf16[32,32,256]{2,1,0:T(8,128)(2,1)S(1)}, u32[]{:S(2)}, u32[]{:S(2)}) async-start(bf16[32,32,256]{2,1,0:T(8,128)(2,1)} %broadcast_in_dim.50), calls=%async_computation.5 | async-start | bytes 1048576 | tf_op jit(solution)/shard_map/all_to_all | solution.py:20
  148.0 0.6 bitcast_subtract_fusion
  148.7 10.9 %all-to-all-done.4 = bf16[32,32,256]{2,1,0:T(8,128)(2,1)S(1)} async-done(((bf16[32,32,256]{2,1,0:T(8,128)(2,1)}), bf16[32,32,256]{2,1,0:T(8,128)(2,1)S(1)}, u32[]{:S(2)}, u32[]{:S(2)}) %all-to-all-start.4) | async-done | bytes 524320 | tf_op jit(solution)/shard_map/all_to_all | solution.py:20
  159.5 1.1 bitcast_convert_fusion
  160.6 0.0 reduce-scatter.2.cloned.1.call-done
  (12 shorter events, 0.1 us)
Async XLA Ops:
  8.0 1.0 copy-start
  8.0 14.3 %copy-start.2 = (s32[16,64]{1,0:T(8,128)S(1)}, s32[16,64]{1,0:T(8,128)}, u32[]{:S(2)}) copy-start(s32[16,64]{1,0:T(8,128)} %param.7) | copy-start | bytes 12292
  8.0 14.6 %copy-start.3 = (s32[2048]{0:T(1024)S(1)}, s32[2048]{0:T(1024)}, u32[]{:S(2)}) copy-start(s32[2048]{0:T(1024)} %param.8) | copy-start | bytes 24580
  8.0 28.5 %copy-start.1 = (bf16[2048,256]{1,0:T(8,128)(2,1)S(1)}, bf16[2048,256]{1,0:T(8,128)(2,1)}, u32[]{:S(2)}) copy-start(bf16[2048,256]{1,0:T(8,128)(2,1)} %user_ref.3) | copy-start | bytes 3145732
  8.0 68.9 %all-gather.2.cloned.1.call-start = ((), (), s32[]{:S(2)}) async-start(), calls=%async_computation.6 | async-start | bytes 2162688 | tf_op jit(solution)/shard_map/all_gather | solution.py:103
  11.8 24.8 %all-to-all-start = ((bf16[32,32,384]{2,1,0:T(8,128)(2,1)}), bf16[32,32,384]{2,1,0:T(8,128)(2,1)S(1)}, u32[]{:S(2)}, u32[]{:S(2)}) async-start(bf16[32,32,384]{2,1,0:T(8,128)(2,1)} %broadcast_in_dim.21), calls=%async_computation | async-start | bytes 1572864 | tf_op jit(solution)/shard_map/all_to_all | solution.py:20
  22.2 138.4 %reduce-scatter.2.cloned.1.call-start = ((), (), s32[]{:S(2)}) async-start(), calls=%async_computation.7 | async-start | bytes 2228224 | tf_op jit(solution)/shard_map/reduce_scatter | solution.py:154
  80.9 16.7 %all-to-all-start.2 = ((bf16[32,32,256]{2,1,0:T(8,128)(2,1)}), bf16[32,32,256]{2,1,0:T(8,128)(2,1)S(1)}, u32[]{:S(2)}, u32[]{:S(2)}) async-start(bf16[32,32,256]{2,1,0:T(8,128)(2,1)} %bitcast.5), calls=%async_computation.2 | async-start | bytes 1048576 | tf_op jit(solution)/shard_map/all_to_all | solution.py:159
  136.2 23.4 %all-to-all-start.4 = ((bf16[32,32,256]{2,1,0:T(8,128)(2,1)}), bf16[32,32,256]{2,1,0:T(8,128)(2,1)S(1)}, u32[]{:S(2)}, u32[]{:S(2)}) async-start(bf16[32,32,256]{2,1,0:T(8,128)(2,1)} %broadcast_in_dim.50), calls=%async_computation.5 | async-start | bytes 1048576 | tf_op jit(solution)/shard_map/all_to_all | solution.py:20
Sparse Core Ops, SparseCore 0:
  12.0 64.8 all-gather.1
Sparse Core Ops, SparseCore 1:
  71.6 70.5 reduce-scatter.1

commit v5 on v4

--- a/solution.py
+++ b/solution.py
@@ -10,7 +10,6 @@
 STEP = 1024
 NEG = -1e30
 FLOOR = -1e29
-PIECES = 3
 NT = (((1,), (1,)), ((), ()))
 f32 = jnp.float32
 bf16 = jnp.bfloat16
@@ -33,7 +32,7 @@
     return lax.broadcasted_iota(jnp.int32, raw.shape, 0) == pos_ref[...]
 
 
-def forward(item_ref, user_ref, mask_ref, pos_ref, lse_ref, own_ref, split_ref):
+def forward(item_ref, user_ref, mask_ref, pos_ref, lse_ref, own_ref, below_ref):
     step = pl.program_id(0)
     raw, kept = logits_of(item_ref, user_ref, mask_ref)
     here = (pos_ref[...] >= 0) & (pos_ref[...] < raw.shape[0])
@@ -46,17 +45,13 @@
         row = step * (STEP // BU) + h
         lse_ref[pl.ds(row, 1), :] = lse[:, h * BU : (h + 1) * BU]
         own_ref[pl.ds(row, 1), :] = pos[:, h * BU : (h + 1) * BU]
-    rest = jnp.where(here, pos, 0.0)
-    width = split_ref.shape[1]
-    for k in range(PIECES):
-        piece = rest.astype(bf16).astype(f32)
-        rest = rest - piece
-        for h in range(STEP // width):
-            row = k * (split_ref.shape[0] // PIECES) + step * (STEP // width) + h
-            split_ref[pl.ds(row, 1), :] = piece[:, h * width : (h + 1) * width]
+    below = jnp.where(here, lse - pos, 0.0)
+    width = below_ref.shape[1]
+    for h in range(STEP // width):
+        below_ref[pl.ds(step * (STEP // width) + h, 1), :] = below[:, h * width : (h + 1) * width]
 
 
-def backward(item_ref, user_ref, mask_ref, pos_ref, lses_ref, own_ref, grad_ref, high_ref, total_ref, item_t, weight_ref, sums):
+def backward(item_ref, user_ref, mask_ref, pos_ref, lses_ref, own_ref, owner_ref, grad_ref, high_ref, gap_ref, item_t, total_ref, weight_ref, sums):
     step = pl.program_id(0)
     width = user_ref.shape[1]
 
@@ -66,6 +61,8 @@
         peak = jnp.max(lse, axis=0)
         total = peak + jnp.log(jnp.sum(jnp.exp(lse - peak[None]), axis=0))
         total_ref[...] = total
+        at_owner = lax.broadcasted_iota(jnp.int32, lse.shape, 0) == owner_ref[...][None]
+        gap_ref[...] = total - jnp.sum(jnp.where(at_owner, lse, 0.0), axis=0)
         weight_ref[...] = jnp.exp(own_ref[...] - total) - 1.0
         item_t[...] = item_ref[:, :width].astype(f32).T.astype(bf16)
         sums[...] = jnp.zeros_like(sums)
@@ -106,6 +103,7 @@
     taken = jnp.any(samples[None] == ids[:, None, None], axis=2)
     mask = jnp.repeat(jnp.where(taken, 0.0, NEG).astype(f32), BU, axis=1)
     pos_row = (pos_item - shard * rows).reshape(1, users)
+    owner = (pos_item // rows).reshape(blocks, BU)
 
     in_specs = [
         pl.BlockSpec((rows, width + CL), lambda i: (0, 0)),
@@ -115,24 +113,24 @@
     ]
     params = pltpu.CompilerParams(vmem_limit_bytes=48 << 20)
     table = pl.BlockSpec((blocks, BU), lambda i: (0, 0))
-    pieces = PIECES * users // width
-    lse, own_pos, split = pl.pallas_call(
+    lines = users // width
+    lse, own_pos, below = pl.pallas_call(
         forward,
         grid=(steps,),
         in_specs=in_specs,
-        out_specs=[table, table, pl.BlockSpec((pieces, width), lambda i: (0, 0))],
+        out_specs=[table, table, pl.BlockSpec((lines, width), lambda i: (0, 0))],
         out_shape=[
             jax.ShapeDtypeStruct((blocks, BU), f32),
             jax.ShapeDtypeStruct((blocks, BU), f32),
-            jax.ShapeDtypeStruct((pieces, width), f32),
+            jax.ShapeDtypeStruct((lines, width), f32),
         ],
         compiler_params=params,
     )(items, user_emb, mask, pos_row)
     lses = spread(lse, "items", shards)
-    grad, high, total = pl.pallas_call(
+    grad, high, gap = pl.pallas_call(
         backward,
         grid=(steps,),
-        in_specs=in_specs + [pl.BlockSpec((shards, blocks, BU), lambda i: (0, 0, 0)), table],
+        in_specs=in_specs + [pl.BlockSpec((shards, blocks, BU), lambda i: (0, 0, 0)), table, table],
         out_specs=[
             pl.BlockSpec((STEP, width), lambda i: (i, 0)),
             pl.BlockSpec((rows, 2 * width), lambda i: (0, 0)),
@@ -146,23 +144,25 @@
         scratch_shapes=[
             pltpu.VMEM((width, rows), bf16),
             pltpu.VMEM((blocks, BU), f32),
+            pltpu.VMEM((blocks, BU), f32),
             pltpu.VMEM((rows, width), f32),
         ],
         compiler_params=params,
-    )(items, user_emb, mask, pos_row, lses, own_pos)
+    )(items, user_emb, mask, pos_row, lses, own_pos, owner)
 
     user_grad = lax.psum_scatter(grad, "items", scatter_dimension=0, tiled=True)
 
     part = lax.dot_general(feats, high, (((0,), (0,)), ((), ())), preferred_element_type=f32)
     part = (part[:, :width] + part[:, width:]).astype(bf16)
     cut = part.shape[0] // group
+    part, below = lax.optimization_barrier((part, below.astype(bf16)))
     part = lax.all_to_all(part.reshape(group, cut, width), "users", 0, 0)
     part = jnp.sum(part.astype(f32), axis=0).astype(bf16)
-    both = spread(jnp.concatenate([part, split.astype(bf16)], axis=0), "items", shards)
+    both = spread(jnp.concatenate([part, below], axis=0), "items", shards)
     both = jnp.sum(both.astype(f32), axis=0)
-    weight_grad = spread(both[:cut].astype(bf16), "users", group).reshape(group * cut, width).astype(f32)
-    pos_logit = jnp.sum(both[cut:].reshape(PIECES, users), axis=0)
-    user_loss = total.reshape(users) - pos_logit
+    user_loss = gap.reshape(users) + both[cut:].reshape(users)
+    part, user_loss = lax.optimization_barrier((both[:cut].astype(bf16), user_loss))
+    weight_grad = spread(part, "users", group).reshape(group * cut, width).astype(f32)
     return user_loss, user_grad, weight_grad
 
 

time: 169 us -> 160 us (0.947)
  blocking collectives: 62.3 us -> 94.6 us
  waiting for transfers between devices: 42.4 us -> 19.9 us
  starting transfers between devices: 27.4 us -> 10.5 us
    all_to_all x0 -> x1, blocking collectives: none -> 16.5 us  [body(): part = lax.all_to_all(part.reshape(group, cut, width), 'users', 0, 0)]
    all_to_all x2 -> x3, blocking collectives: 62.3 us -> 78.2 us  [spread(): return lax.all_to_all(jnp.broadcast_to(x[None], (n,) + x.shape), axis, 0, 0)]
    all_to_all x2 -> x1, starting transfers between devices: 22.3 us -> 10.4 us  [spread(): return lax.all_to_all(jnp.broadcast_to(x[None], (n,) + x.shape), axis, 0, 0)]
    all_to_all x1 -> x0, waiting for transfers between devices: 11.5 us -> none  [body(): part = lax.all_to_all(part.reshape(group, cut, width), 'users', 0, 0)]
    all_to_all x2 -> x1, waiting for transfers between devices: 24.7 us -> 13.8 us  [spread(): return lax.all_to_all(jnp.broadcast_to(x[None], (n,) + x.shape), axis, 0, 0)]
    all_to_all x1 -> x0, starting transfers between devices: 5.11 us -> none  [body(): part = lax.all_to_all(part.reshape(group, cut, width), 'users', 0, 0)]
  transfers between devices with their start and end apart: 5 -> 3, of which waited for: 4 -> 2; matrix products, arithmetic and copies ran while one was open for 6% -> 5% of each run, Pallas kernels for 6% -> 6%
where the time goes in v5:
time: 160 us; the launch traced here: 159 us
  blocking collectives  94.6 us (59%)
  waiting for transfers between devices  19.9 us (12%)
  between operations  15.6 us (10%)
  starting transfers between devices  10.5 us (7%)
  Pallas kernels  10.1 us (6%)
  matrix products  3.88 us (2%)
  local copies, waits for them, and re-layouts  2.42 us (2%)
  other arithmetic  2.28 us (1%)
    all_to_all x3, blocking collectives, spread(): return lax.all_to_all(jnp.broadcast_to(x[None], (n,) + x.shape), axis, 0, 0)  78.2 us
    all_to_all x1, blocking collectives, body(): part = lax.all_to_all(part.reshape(group, cut, width), 'users', 0, 0)  16.5 us
    all_to_all x1, waiting for transfers between devices, spread(): return lax.all_to_all(jnp.broadcast_to(x[None], (n,) + x.shape), axis, 0, 0)  13.8 us
    all_to_all x1, starting transfers between devices, spread(): return lax.all_to_all(jnp.broadcast_to(x[None], (n,) + x.shape), axis, 0, 0)  10.4 us
    pallas_call x1, Pallas kernels, body(): pl.pallas_call(backward, grid=(steps,), in_specs=in_specs + [pl.BlockSpec...  6 us
    all_gather x1, waiting for transfers between devices, body(): feats = lax.all_gather(item_feat, 'users', axis=0, tiled=True)  5.44 us
    pallas_call x1, Pallas kernels, body(): pl.pallas_call(forward, grid=(steps,), in_specs=in_specs, out_specs=[tabl...  4.11 us
  transfers between devices with their start and end apart: 3, of which 2 were waited for; matrix products, arithmetic and copies ran while one was open for 5% of the time, Pallas kernels for 6%

profile of v5, /device:TPU:1, one launch (start us, length us, event | category | flops | bytes accessed | tf_op | source)
XLA Modules:
  0.0 159.4 jit_solution(14655001963135145244)
XLA Ops:
  8.0 0.0 copy-start
  8.0 0.0 copy-start.3
  8.0 0.0 copy-start.2
  8.0 0.0 copy-start.1
  8.0 0.0 all-gather.2.cloned.1.call-start
  8.1 0.7 all-gather.2.cloned.1.call-update
  8.8 0.3 copy-done
  9.0 1.0 convolution_convert_fusion
  10.1 0.7 broadcast_in_dim.20
  10.8 1.0 broadcast_in_dim.21
  11.8 10.4 %all-to-all-start = ((bf16[32,32,384]{2,1,0:T(8,128)(2,1)}), bf16[32,32,384]{2,1,0:T(8,128)(2,1)S(1)}, u32[]{:S(2)}, u32[]{:S(2)}) async-start(bf16[32,32,384]{2,1,0:T(8,128)(2,1)} %broadcast_in_dim.21), calls=%async_computation | async-start | bytes 1572864 | tf_op jit(solution)/shard_map/all_to_all | solution.py:19
  22.2 0.0 reduce-scatter.2.cloned.1.call-start
  22.3 0.0 copy-done.3
  22.3 0.3 compare_reduce_fusion
  22.6 0.1 copy.10
  22.7 0.0 copy-done.2
  22.7 0.1 broadcast_bitcast_fusion.mask_ref
  22.8 13.8 %all-to-all-done = bf16[32,32,384]{2,1,0:T(8,128)(2,1)S(1)} async-done(((bf16[32,32,384]{2,1,0:T(8,128)(2,1)}), bf16[32,32,384]{2,1,0:T(8,128)(2,1)S(1)}, u32[]{:S(2)}, u32[]{:S(2)}) %all-to-all-start) | async-done | bytes 786464 | tf_op jit(solution)/shard_map/all_to_all | solution.py:19
  36.6 0.0 copy-done.1
  36.6 4.1 %shard_map.85 = (f32[16,128]{1,0:T(8,128)S(1)}, f32[16,128]{1,0:T(8,128)S(1)}, f32[8,256]{1,0:T(8,128)S(1)}) custom-call(bf16[1024,384]{1,0:T(8,128)(2,1)S(1)} %bitcast.21, bf16[2048,256]{1,0:T(8,128)(2,1)S(1)} %copy-done.1, f32[8,2048]{1,0:T(8,128)S(1)} %broadcast_bitcast_fusion.mask_ref, s32[1,2048]{1,0:T(1,128)S(1)} %bitcast.23), custom_call_target="tpu_custom_call" | custom-call | tf_op jit(solution)/shard_map/pallas_call | solution.py:117
  40.7 24.8 %all_to_all.25.lses_ref = f32[16,16,128]{2,1,0:T(8,128)S(1)} all-to-all(f32[16,16,128]{2,1,0:T(8,128)S(1)} %broadcast_in_dim.25), channel_id=1, replica_groups=mesh['users'=32,'items'=16] {'items'}, dimensions={0} | all-to-all | bytes 262144 | tf_op jit(solution)/shard_map/all_to_all | solution.py:19
  65.4 6.0 %shard_map.86 = (f32[2048,256]{1,0:T(8,128)}, bf16[1024,512]{1,0:T(8,128)(2,1)S(1)}, f32[16,128]{1,0:T(8,128)S(1)}) custom-call(bf16[1024,384]{1,0:T(8,128)(2,1)S(1)} %bitcast.22, bf16[2048,256]{1,0:T(8,128)(2,1)S(1)} %copy-done.1, f32[8,2048]{1,0:T(8,128)S(1)} %broadcast_bitcast_fusion.mask_ref, s32[1,2048]{1,0:T(1,128)S(1)} %bitcast.24, ...), custom_call_target="tpu_custom_call" | custom-call | tf_op jit(solution)/shard_map/pallas_call | solution.py:130
  71.4 0.0 reduce-scatter.2.cloned.1.call-update
  71.5 5.4 %all-gather.2.cloned.1.call-done = bf16[1024,1024]{1,0:T(8,128)(2,1)} async-done(((bf16[32,1024]{1,0:T(8,128)(2,1)}), bf16[1024,1024]{1,0:T(8,128)(2,1)}) %all-gather.2.cloned.1.call-update) | async-done | bytes 2097168 | tf_op jit(solution)/shard_map/all_gather | solution.py:100
  76.9 2.9 %convolution_bitcast_fusion = f32[1024,512]{0,1:T(8,128)S(1)} fusion(bf16[1024,512]{1,0:T(8,128)(2,1)S(1)} %get-tuple-element.15, bf16[1024,1024]{1,0:T(8,128)(2,1)} %all-gather.2.cloned.1.call-done), kind=kOutput, calls=%fused_computation | convolution fusion | flops 1073741824 | bytes 5242880 | tf_op jit(solution)/shard_map/dot_general | solution.py:155
  79.8 0.1 fusion
  79.9 0.2 copy.11
  80.1 16.5 %all_to_all.26 = bf16[32,32,256]{2,1,0:T(8,128)(2,1)S(1)} all-to-all(bf16[32,32,256]{2,1,0:T(8,128)(2,1)S(1)} %bitcast.25), channel_id=1, replica_groups=mesh['users'=32,'items'=16] {'users'}, dimensions={0} | all-to-all | bytes 1048576 | tf_op jit(solution)/shard_map/all_to_all | solution.py:159
  96.6 0.1 reduce_sum.21
  96.7 31.0 %all_to_all.27 = bf16[16,40,256]{2,1,0:T(8,128)(2,1)S(1)} all-to-all(bf16[16,40,256]{2,1,0:T(8,128)(2,1)S(1)} %broadcast_in_dim.26), channel_id=1, replica_groups=mesh['users'=32,'items'=16] {'items'}, dimensions={0} | all-to-all | bytes 655360 | tf_op jit(solution)/shard_map/all_to_all | solution.py:19
  127.7 0.1 convert_reduce_fusion
  127.8 0.6 bitcast_add_fusion
  128.5 22.4 %all_to_all.28 = bf16[32,32,256]{2,1,0:T(8,128)(2,1)S(1)} all-to-all(bf16[32,32,256]{2,1,0:T(8,128)(2,1)S(1)} %broadcast_in_dim.50), channel_id=1, replica_groups=mesh['users'=32,'items'=16] {'users'}, dimensions={0} | all-to-all | bytes 1048576 | tf_op jit(solution)/shard_map/all_to_all | solution.py:19
  150.9 1.1 bitcast_convert_fusion
  152.0 0.0 reduce-scatter.2.cloned.1.call-done
  (12 shorter events, 0.1 us)
Async XLA Ops:
  8.0 1.0 copy-start
  8.0 14.3 %copy-start.3 = (s32[16,64]{1,0:T(8,128)S(1)}, s32[16,64]{1,0:T(8,128)}, u32[]{:S(2)}) copy-start(s32[16,64]{1,0:T(8,128)} %param.7) | copy-start | bytes 12292
  8.0 14.6 %copy-start.2 = (s32[2048]{0:T(1024)S(1)}, s32[2048]{0:T(1024)}, u32[]{:S(2)}) copy-start(s32[2048]{0:T(1024)} %param.8) | copy-start | bytes 24580
  8.0 28.5 %copy-start.1 = (bf16[2048,256]{1,0:T(8,128)(2,1)S(1)}, bf16[2048,256]{1,0:T(8,128)(2,1)}, u32[]{:S(2)}) copy-start(bf16[2048,256]{1,0:T(8,128)(2,1)} %user_ref.3) | copy-start | bytes 3145732
  8.0 68.9 %all-gather.2.cloned.1.call-start = ((), (), s32[]{:S(2)}) async-start(), calls=%async_computation.6 | async-start | bytes 2162688 | tf_op jit(solution)/shard_map/all_gather | solution.py:100
  11.8 24.8 %all-to-all-start = ((bf16[32,32,384]{2,1,0:T(8,128)(2,1)}), bf16[32,32,384]{2,1,0:T(8,128)(2,1)S(1)}, u32[]{:S(2)}, u32[]{:S(2)}) async-start(bf16[32,32,384]{2,1,0:T(8,128)(2,1)} %broadcast_in_dim.21), calls=%async_computation | async-start | bytes 1572864 | tf_op jit(solution)/shard_map/all_to_all | solution.py:19
  22.2 129.7 %reduce-scatter.2.cloned.1.call-start = ((), (), s32[]{:S(2)}) async-start(), calls=%async_computation.7 | async-start | bytes 2228224 | tf_op jit(solution)/shard_map/reduce_scatter | solution.py:153
Sparse Core Ops, SparseCore 0:
  12.0 64.8 all-gather.1
Sparse Core Ops, SparseCore 1:
  71.6 66.7 reduce-scatter.1

commit v6 on v3

--- a/solution.py
+++ b/solution.py
@@ -7,7 +7,7 @@
 
 CL = 128
 BU = 128
-STEP = 256
+STEP = 1024
 NEG = -1e30
 FLOOR = -1e29
 NT = (((1,), (1,)), ((), ()))
@@ -48,17 +48,17 @@
         stat_ref[pl.ds(blocks + row, 1), :] = pos[:, h * BU : (h + 1) * BU]
 
 
-def backward(item_ref, user_ref, mask_ref, pos_ref, stat_ref, grad_ref, high_ref, loss_ref, item_t, total_ref, weight_ref, sums):
+def backward(item_ref, user_ref, mask_ref, pos_ref, stats_ref, grad_ref, high_ref, loss_ref, item_t, total_ref, weight_ref, sums):
     step = pl.program_id(0)
     width = user_ref.shape[1]
     blocks = loss_ref.shape[0]
 
     @pl.when(step == 0)
     def _():
-        lse = stat_ref[:, :blocks, :]
+        lse = stats_ref[:, :blocks, :]
         peak = jnp.max(lse, axis=0)
         total = peak + jnp.log(jnp.sum(jnp.exp(lse - peak[None]), axis=0))
-        pos = jnp.max(stat_ref[:, blocks:, :], axis=0)
+        pos = jnp.max(stats_ref[:, blocks:, :], axis=0)
         total_ref[...] = total
         loss_ref[...] = total - pos
         weight_ref[...] = jnp.exp(pos - total) - 1.0
@@ -92,8 +92,9 @@
     users, blocks = user_emb.shape[0], samples.shape[0]
     steps = users // STEP
 
-    own_emb = jnp.dot(item_feat, tower_w, preferred_element_type=f32).astype(bf16)
-    packed = jnp.concatenate([own_emb, jnp.broadcast_to(item_bias[:, None], (own, CL))], axis=1)
+    feat, bias = lax.optimization_barrier((item_feat, jnp.broadcast_to(item_bias[:, None], (own, CL))))
+    own_emb = jnp.dot(feat, tower_w, preferred_element_type=f32).astype(bf16)
+    packed = jnp.concatenate([own_emb, bias], axis=1)
     items = spread(packed, "users", group).reshape(rows, width + CL)
     feats = lax.all_gather(item_feat, "users", axis=0, tiled=True)
 
@@ -108,7 +109,7 @@
         pl.BlockSpec((clus, STEP), lambda i: (0, i)),
         pl.BlockSpec((1, STEP), lambda i: (0, i)),
     ]
-    params = pltpu.CompilerParams(vmem_limit_bytes=40 << 20)
+    params = pltpu.CompilerParams(vmem_limit_bytes=48 << 20)
     stat = pl.pallas_call(
         forward,
         grid=(steps,),
@@ -128,7 +129,7 @@
             pl.BlockSpec((blocks, BU), lambda i: (0, 0)),
         ],
         out_shape=[
-            jax.ShapeDtypeStruct((users, width), f32),
+            pltpu.HBM((users, width), f32),
             jax.ShapeDtypeStruct((rows, 2 * width), bf16),
             jax.ShapeDtypeStruct((blocks, BU), f32),
         ],
@@ -150,7 +151,6 @@
     part = jnp.sum(part.astype(f32), axis=0).astype(bf16)
     part = jnp.sum(spread(part, "items", shards).astype(f32), axis=0).astype(bf16)
     weight_grad = spread(part, "users", group).reshape(group * cut, width).astype(f32)
-
     return loss.reshape(users), user_grad, weight_grad
 
 

time: 165 us -> 158 us (0.958)
  the two profiles are of different devices: /device:TPU:2 before, /device:TPU:1 now
where the time goes in v6:
time: 158 us; the launch traced here: 156 us
  blocking collectives  93.4 us (59%)
  waiting for transfers between devices  18.8 us (12%)
  between operations  15.6 us (10%)
  starting transfers between devices  10.5 us (7%)
  Pallas kernels  10 us (6%)
  matrix products  3.89 us (2%)
  local copies, waits for them, and re-layouts  2.14 us (1%)
  other arithmetic  1.65 us (1%)
    all_to_all x3, blocking collectives, spread(): return lax.all_to_all(jnp.broadcast_to(x[None], (n,) + x.shape), axis, 0, 0)  77 us
    all_to_all x1, blocking collectives, body(): part = lax.all_to_all(part.reshape(group, cut, width), 'users', 0, 0)  16.5 us
    all_to_all x1, waiting for transfers between devices, spread(): return lax.all_to_all(jnp.broadcast_to(x[None], (n,) + x.shape), axis, 0, 0)  13.8 us
    all_to_all x1, starting transfers between devices, spread(): return lax.all_to_all(jnp.broadcast_to(x[None], (n,) + x.shape), axis, 0, 0)  10.4 us
    pallas_call x1, Pallas kernels, body(): pl.pallas_call(backward, grid=(steps,), in_specs=in_specs + [pl.BlockSpec...  5.94 us
    all_gather x1, waiting for transfers between devices, body(): feats = lax.all_gather(item_feat, 'users', axis=0, tiled=True)  4.28 us
    pallas_call x1, Pallas kernels, body(): pl.pallas_call(forward, grid=(steps,), in_specs=in_specs, out_specs=pl.Bl...  4.07 us
  transfers between devices with their start and end apart: 3, of which 2 were waited for; matrix products, arithmetic and copies ran while one was open for 5% of the time, Pallas kernels for 6%

profile of v6, /device:TPU:1, one launch (start us, length us, event | category | flops | bytes accessed | tf_op | source)
XLA Modules:
  0.0 156.0 jit_solution(15519729921464788883)
XLA Ops:
  8.0 0.0 copy-start
  8.0 0.0 copy-start.2
  8.0 0.0 copy-start.3
  8.0 0.0 copy-start.1
  8.0 0.0 all-gather.2.cloned.1.call-start
  8.1 0.7 all-gather.2.cloned.1.call-update
  8.8 0.7 broadcast_in_dim.20
  9.5 0.0 copy-done
  9.5 1.0 convolution_convert_fusion
  10.6 1.0 broadcast_in_dim.21
  11.5 10.4 %all-to-all-start = ((bf16[32,32,384]{2,1,0:T(8,128)(2,1)}), bf16[32,32,384]{2,1,0:T(8,128)(2,1)S(1)}, u32[]{:S(2)}, u32[]{:S(2)}) async-start(bf16[32,32,384]{2,1,0:T(8,128)(2,1)} %broadcast_in_dim.21), calls=%async_computation | async-start | bytes 1572864 | tf_op jit(solution)/shard_map/all_to_all | solution.py:19
  22.0 0.0 reduce-scatter.2.cloned.1.call-start
  22.0 0.0 copy-done.2
  22.0 0.3 compare_reduce_fusion
  22.3 0.1 copy.10
  22.4 0.0 copy-done.3
  22.4 0.1 broadcast_bitcast_fusion.mask_ref
  22.5 13.8 %all-to-all-done = bf16[32,32,384]{2,1,0:T(8,128)(2,1)S(1)} async-done(((bf16[32,32,384]{2,1,0:T(8,128)(2,1)}), bf16[32,32,384]{2,1,0:T(8,128)(2,1)S(1)}, u32[]{:S(2)}, u32[]{:S(2)}) %all-to-all-start) | async-done | bytes 786464 | tf_op jit(solution)/shard_map/all_to_all | solution.py:19
  36.3 0.0 copy-done.1
  36.3 4.1 %shard_map.85 = f32[32,128]{1,0:T(8,128)S(1)} custom-call(bf16[1024,384]{1,0:T(8,128)(2,1)S(1)} %bitcast.15, bf16[2048,256]{1,0:T(8,128)(2,1)S(1)} %copy-done.1, f32[8,2048]{1,0:T(8,128)S(1)} %broadcast_bitcast_fusion.mask_ref, s32[1,2048]{1,0:T(1,128)S(1)} %bitcast.17), custom_call_target="tpu_custom_call" | custom-call | tf_op jit(solution)/shard_map/pallas_call | solution.py:113
  40.4 26.3 %all_to_all.25.stats_ref = f32[16,32,128]{2,1,0:T(8,128)S(1)} all-to-all(f32[16,32,128]{2,1,0:T(8,128)S(1)} %broadcast_in_dim.25), channel_id=1, replica_groups=mesh['users'=32,'items'=16] {'items'}, dimensions={0} | all-to-all | bytes 524288 | tf_op jit(solution)/shard_map/all_to_all | solution.py:19
  66.7 5.9 %shard_map.86 = (f32[2048,256]{1,0:T(8,128)}, bf16[1024,512]{1,0:T(8,128)(2,1)S(1)}, f32[16,128]{1,0:T(8,128)}) custom-call(bf16[1024,384]{1,0:T(8,128)(2,1)S(1)} %bitcast.16, bf16[2048,256]{1,0:T(8,128)(2,1)S(1)} %copy-done.1, f32[8,2048]{1,0:T(8,128)S(1)} %broadcast_bitcast_fusion.mask_ref, s32[1,2048]{1,0:T(1,128)S(1)} %bitcast.18, ...), custom_call_target="tpu_custom_call" | custom-call | tf_op jit(solution)/shard_map/pallas_call | solution.py:122
  72.6 0.0 reduce-scatter.2.cloned.1.call-update
  72.6 4.3 %all-gather.2.cloned.1.call-done = bf16[1024,1024]{1,0:T(8,128)(2,1)} async-done(((bf16[32,1024]{1,0:T(8,128)(2,1)}), bf16[1024,1024]{1,0:T(8,128)(2,1)}) %all-gather.2.cloned.1.call-update) | async-done | bytes 2097168 | tf_op jit(solution)/shard_map/all_gather | solution.py:99
  76.9 2.9 %convolution_bitcast_fusion = f32[1024,512]{0,1:T(8,128)S(1)} fusion(bf16[1024,512]{1,0:T(8,128)(2,1)S(1)} %get-tuple-element.12, bf16[1024,1024]{1,0:T(8,128)(2,1)} %all-gather.2.cloned.1.call-done), kind=kOutput, calls=%fused_computation | convolution fusion | flops 1073741824 | bytes 5242880 | tf_op jit(solution)/shard_map/dot_general | solution.py:147
  79.8 0.1 fusion
  79.9 0.2 copy.11
  80.1 16.5 %all_to_all.26 = bf16[32,32,256]{2,1,0:T(8,128)(2,1)S(1)} all-to-all(bf16[32,32,256]{2,1,0:T(8,128)(2,1)S(1)} %bitcast.19), channel_id=1, replica_groups=mesh['users'=32,'items'=16] {'users'}, dimensions={0} | all-to-all | bytes 1048576 | tf_op jit(solution)/shard_map/all_to_all | solution.py:150
  96.6 0.1 reduce_sum.24
  96.7 27.7 %all_to_all.27 = bf16[16,32,256]{2,1,0:T(8,128)(2,1)S(1)} all-to-all(bf16[16,32,256]{2,1,0:T(8,128)(2,1)S(1)} %broadcast_in_dim.26), channel_id=1, replica_groups=mesh['users'=32,'items'=16] {'items'}, dimensions={0} | all-to-all | bytes 524288 | tf_op jit(solution)/shard_map/all_to_all | solution.py:19
  124.5 0.1 broadcast_in_dim.50
  124.5 23.0 %all_to_all.28 = bf16[32,32,256]{2,1,0:T(8,128)(2,1)S(1)} all-to-all(bf16[32,32,256]{2,1,0:T(8,128)(2,1)S(1)} %broadcast_in_dim.50), channel_id=1, replica_groups=mesh['users'=32,'items'=16] {'users'}, dimensions={0} | all-to-all | bytes 1048576 | tf_op jit(solution)/shard_map/all_to_all | solution.py:19
  147.5 1.1 bitcast_convert_fusion
  148.6 0.0 reduce-scatter.2.cloned.1.call-done
  (7 shorter events, 0.1 us)
Async XLA Ops:
  8.0 1.5 copy-start
  8.0 14.0 %copy-start.2 = (s32[16,64]{1,0:T(8,128)S(1)}, s32[16,64]{1,0:T(8,128)}, u32[]{:S(2)}) copy-start(s32[16,64]{1,0:T(8,128)} %param.7) | copy-start | bytes 12292
  8.0 14.4 %copy-start.3 = (s32[2048]{0:T(1024)S(1)}, s32[2048]{0:T(1024)}, u32[]{:S(2)}) copy-start(s32[2048]{0:T(1024)} %param.8) | copy-start | bytes 24580
  8.0 28.3 %copy-start.1 = (bf16[2048,256]{1,0:T(8,128)(2,1)S(1)}, bf16[2048,256]{1,0:T(8,128)(2,1)}, u32[]{:S(2)}) copy-start(bf16[2048,256]{1,0:T(8,128)(2,1)} %user_ref.3) | copy-start | bytes 3145732
  8.0 68.9 %all-gather.2.cloned.1.call-start = ((), (), s32[]{:S(2)}) async-start(), calls=%async_computation.7 | async-start | bytes 2162688 | tf_op jit(solution)/shard_map/all_gather | solution.py:99
  11.5 24.8 %all-to-all-start = ((bf16[32,32,384]{2,1,0:T(8,128)(2,1)}), bf16[32,32,384]{2,1,0:T(8,128)(2,1)S(1)}, u32[]{:S(2)}, u32[]{:S(2)}) async-start(bf16[32,32,384]{2,1,0:T(8,128)(2,1)} %broadcast_in_dim.21), calls=%async_computation | async-start | bytes 1572864 | tf_op jit(solution)/shard_map/all_to_all | solution.py:19
  22.0 126.6 %reduce-scatter.2.cloned.1.call-start = ((), (), s32[]{:S(2)}) async-start(), calls=%async_computation.6 | async-start | bytes 2228224 | tf_op jit(solution)/shard_map/reduce_scatter | solution.py:145
Sparse Core Ops, SparseCore 0:
  12.0 64.8 all-gather.1
Sparse Core Ops, SparseCore 1:
  72.7 69.5 reduce-scatter.1

commit v7 on v6

--- a/solution.py
+++ b/solution.py
@@ -1,3 +1,5 @@
+import functools
+
 import jax
 import jax.numpy as jnp
 from jax import lax
@@ -19,13 +21,11 @@
     return lax.all_to_all(jnp.broadcast_to(x[None], (n,) + x.shape), axis, 0, 0)
 
 
-def logits_of(item_ref, user_ref, mask_ref):
+def logits_of(item_ref, user_ref):
     width = user_ref.shape[1]
     raw = lax.dot_general(item_ref[:, :width], user_ref[...], NT, preferred_element_type=f32)
     bias = item_ref[:, width:].astype(f32)
-    raw = raw + jnp.concatenate([bias] * (STEP // CL), axis=1)
-    parts = [raw[c * CL : (c + 1) * CL] + mask_ref[c : c + 1, :] for c in range(raw.shape[0] // CL)]
-    return raw, jnp.concatenate(parts, axis=0)
+    return raw + jnp.concatenate([bias] * (STEP // CL), axis=1)
 
 
 def at_positive(raw, pos_ref):
@@ -34,12 +34,17 @@
 
 def forward(item_ref, user_ref, mask_ref, pos_ref, stat_ref):
     step = pl.program_id(0)
-    raw, kept = logits_of(item_ref, user_ref, mask_ref)
+    raw = logits_of(item_ref, user_ref)
+    tiles = [slice(c * CL, (c + 1) * CL) for c in range(raw.shape[0] // CL)]
     here = (pos_ref[...] >= 0) & (pos_ref[...] < raw.shape[0])
     pos = jnp.sum(jnp.where(at_positive(raw, pos_ref), raw, 0.0), axis=0, keepdims=True)
     pos = jnp.where(here, pos, NEG)
-    peak = jnp.maximum(jnp.maximum(jnp.max(kept, axis=0, keepdims=True), pos), FLOOR)
-    total = jnp.sum(jnp.exp(kept - peak), axis=0, keepdims=True) + jnp.exp(pos - peak)
+    tops = [jnp.max(raw[t], axis=0, keepdims=True) + mask_ref[c : c + 1, :] for c, t in enumerate(tiles)]
+    peak = functools.reduce(jnp.maximum, tops, jnp.maximum(pos, FLOOR))
+    total = jnp.exp(pos - peak)
+    for c, t in enumerate(tiles):
+        part = jnp.sum(jnp.exp(raw[t] - peak), axis=0, keepdims=True)
+        total = total + jnp.where(mask_ref[c : c + 1, :] == 0.0, part, 0.0)
     lse = jnp.where(total > 0.0, peak + jnp.log(jnp.maximum(total, 1e-37)), NEG)
     blocks = stat_ref.shape[0] // 2
     for h in range(STEP // BU):
@@ -69,8 +74,10 @@
         rows = [ref[pl.ds(step * (STEP // BU) + h, 1), :] for h in range(STEP // BU)]
         return jnp.concatenate(rows, axis=1)
 
-    raw, kept = logits_of(item_ref, user_ref, mask_ref)
-    soft = jnp.exp(kept - row_of(total_ref))
+    raw = logits_of(item_ref, user_ref)
+    shift = row_of(total_ref)
+    tiles = [raw[c * CL : (c + 1) * CL] + (mask_ref[c : c + 1, :] - shift) for c in range(raw.shape[0] // CL)]
+    soft = jnp.exp(jnp.concatenate(tiles, axis=0))
     soft = soft + jnp.where(at_positive(raw, pos_ref), row_of(weight_ref), 0.0)
     soft = soft.astype(bf16)
     sums[...] += jnp.dot(soft, user_ref[...], preferred_element_type=f32)

time: 158 us -> 158 us (level)
  no operation moved by 1% of the time
where the time goes in v7:
time: 158 us; the launch traced here: 156 us
  blocking collectives  93 us (59%)
  waiting for transfers between devices  19.3 us (12%)
  between operations  15.6 us (10%)
  starting transfers between devices  10.5 us (7%)
  Pallas kernels  9.46 us (6%)
  matrix products  3.88 us (2%)
  local copies, waits for them, and re-layouts  2.14 us (1%)
  other arithmetic  1.65 us (1%)
    all_to_all x3, blocking collectives, spread(): return lax.all_to_all(jnp.broadcast_to(x[None], (n,) + x.shape), axis, 0, 0)  76.6 us
    all_to_all x1, blocking collectives, body(): part = lax.all_to_all(part.reshape(group, cut, width), 'users', 0, 0)  16.5 us
    all_to_all x1, waiting for transfers between devices, spread(): return lax.all_to_all(jnp.broadcast_to(x[None], (n,) + x.shape), axis, 0, 0)  13.8 us
    all_to_all x1, starting transfers between devices, spread(): return lax.all_to_all(jnp.broadcast_to(x[None], (n,) + x.shape), axis, 0, 0)  10.4 us
    pallas_call x1, Pallas kernels, body(): pl.pallas_call(backward, grid=(steps,), in_specs=in_specs + [pl.BlockSpec...  5.71 us
    all_gather x1, waiting for transfers between devices, body(): feats = lax.all_gather(item_feat, 'users', axis=0, tiled=True)  4.83 us
    pallas_call x1, Pallas kernels, body(): pl.pallas_call(forward, grid=(steps,), in_specs=in_specs, out_specs=pl.Bl...  3.75 us
  transfers between devices with their start and end apart: 3, of which 2 were waited for; matrix products, arithmetic and copies ran while one was open for 5% of the time, Pallas kernels for 6%

profile of v7, /device:TPU:1, one launch (start us, length us, event | category | flops | bytes accessed | tf_op | source)
XLA Modules:
  0.0 155.6 jit_solution(14245515421648210431)
XLA Ops:
  8.0 0.0 copy-start
  8.0 0.0 copy-start.2
  8.0 0.0 copy-start.3
  8.0 0.0 copy-start.1
  8.0 0.0 all-gather.2.cloned.1.call-start
  8.1 0.7 all-gather.2.cloned.1.call-update
  8.8 0.7 broadcast_in_dim.20
  9.5 0.0 copy-done
  9.5 1.0 convolution_convert_fusion
  10.6 1.0 broadcast_in_dim.21
  11.5 10.4 %all-to-all-start = ((bf16[32,32,384]{2,1,0:T(8,128)(2,1)}), bf16[32,32,384]{2,1,0:T(8,128)(2,1)S(1)}, u32[]{:S(2)}, u32[]{:S(2)}) async-start(bf16[32,32,384]{2,1,0:T(8,128)(2,1)} %broadcast_in_dim.21), calls=%async_computation | async-start | bytes 1572864 | tf_op jit(solution)/shard_map/all_to_all | solution.py:21
  22.0 0.0 reduce-scatter.2.cloned.1.call-start
  22.0 0.0 copy-done.2
  22.0 0.3 compare_reduce_fusion
  22.3 0.1 copy.10
  22.4 0.0 copy-done.3
  22.4 0.1 broadcast_bitcast_fusion.mask_ref
  22.5 13.8 %all-to-all-done = bf16[32,32,384]{2,1,0:T(8,128)(2,1)S(1)} async-done(((bf16[32,32,384]{2,1,0:T(8,128)(2,1)}), bf16[32,32,384]{2,1,0:T(8,128)(2,1)S(1)}, u32[]{:S(2)}, u32[]{:S(2)}) %all-to-all-start) | async-done | bytes 786464 | tf_op jit(solution)/shard_map/all_to_all | solution.py:21
  36.3 0.0 copy-done.1
  36.3 3.8 %shard_map.85 = f32[32,128]{1,0:T(8,128)S(1)} custom-call(bf16[1024,384]{1,0:T(8,128)(2,1)S(1)} %bitcast.15, bf16[2048,256]{1,0:T(8,128)(2,1)S(1)} %copy-done.1, f32[8,2048]{1,0:T(8,128)S(1)} %broadcast_bitcast_fusion.mask_ref, s32[1,2048]{1,0:T(1,128)S(1)} %bitcast.17), custom_call_target="tpu_custom_call" | custom-call | tf_op jit(solution)/shard_map/pallas_call | solution.py:120
  40.1 26.3 %all_to_all.25.stats_ref = f32[16,32,128]{2,1,0:T(8,128)S(1)} all-to-all(f32[16,32,128]{2,1,0:T(8,128)S(1)} %broadcast_in_dim.25), channel_id=1, replica_groups=mesh['users'=32,'items'=16] {'items'}, dimensions={0} | all-to-all | bytes 524288 | tf_op jit(solution)/shard_map/all_to_all | solution.py:21
  66.3 5.7 %shard_map.86 = (f32[2048,256]{1,0:T(8,128)}, bf16[1024,512]{1,0:T(8,128)(2,1)S(1)}, f32[16,128]{1,0:T(8,128)}) custom-call(bf16[1024,384]{1,0:T(8,128)(2,1)S(1)} %bitcast.16, bf16[2048,256]{1,0:T(8,128)(2,1)S(1)} %copy-done.1, f32[8,2048]{1,0:T(8,128)S(1)} %broadcast_bitcast_fusion.mask_ref, s32[1,2048]{1,0:T(1,128)S(1)} %bitcast.18, ...), custom_call_target="tpu_custom_call" | custom-call | tf_op jit(solution)/shard_map/pallas_call | solution.py:129
  72.1 0.0 reduce-scatter.2.cloned.1.call-update
  72.1 4.8 %all-gather.2.cloned.1.call-done = bf16[1024,1024]{1,0:T(8,128)(2,1)} async-done(((bf16[32,1024]{1,0:T(8,128)(2,1)}), bf16[1024,1024]{1,0:T(8,128)(2,1)}) %all-gather.2.cloned.1.call-update) | async-done | bytes 2097168 | tf_op jit(solution)/shard_map/all_gather | solution.py:106
  76.9 2.9 %convolution_bitcast_fusion = f32[1024,512]{0,1:T(8,128)S(1)} fusion(bf16[1024,512]{1,0:T(8,128)(2,1)S(1)} %get-tuple-element.12, bf16[1024,1024]{1,0:T(8,128)(2,1)} %all-gather.2.cloned.1.call-done), kind=kOutput, calls=%fused_computation | convolution fusion | flops 1073741824 | bytes 5242880 | tf_op jit(solution)/shard_map/dot_general | solution.py:154
  79.8 0.1 fusion
  79.9 0.2 copy.11
  80.1 16.5 %all_to_all.26 = bf16[32,32,256]{2,1,0:T(8,128)(2,1)S(1)} all-to-all(bf16[32,32,256]{2,1,0:T(8,128)(2,1)S(1)} %bitcast.19), channel_id=1, replica_groups=mesh['users'=32,'items'=16] {'users'}, dimensions={0} | all-to-all | bytes 1048576 | tf_op jit(solution)/shard_map/all_to_all | solution.py:157
  96.6 0.1 reduce_sum.24
  96.7 26.9 %all_to_all.27 = bf16[16,32,256]{2,1,0:T(8,128)(2,1)S(1)} all-to-all(bf16[16,32,256]{2,1,0:T(8,128)(2,1)S(1)} %broadcast_in_dim.26), channel_id=1, replica_groups=mesh['users'=32,'items'=16] {'items'}, dimensions={0} | all-to-all | bytes 524288 | tf_op jit(solution)/shard_map/all_to_all | solution.py:21
  123.7 0.1 broadcast_in_dim.50
  123.8 23.3 %all_to_all.28 = bf16[32,32,256]{2,1,0:T(8,128)(2,1)S(1)} all-to-all(bf16[32,32,256]{2,1,0:T(8,128)(2,1)S(1)} %broadcast_in_dim.50), channel_id=1, replica_groups=mesh['users'=32,'items'=16] {'users'}, dimensions={0} | all-to-all | bytes 1048576 | tf_op jit(solution)/shard_map/all_to_all | solution.py:21
  147.1 1.1 bitcast_convert_fusion
  148.2 0.0 reduce-scatter.2.cloned.1.call-done
  (7 shorter events, 0.1 us)
Async XLA Ops:
  8.0 1.5 copy-start
  8.0 14.0 %copy-start.2 = (s32[16,64]{1,0:T(8,128)S(1)}, s32[16,64]{1,0:T(8,128)}, u32[]{:S(2)}) copy-start(s32[16,64]{1,0:T(8,128)} %param.7) | copy-start | bytes 12292
  8.0 14.4 %copy-start.3 = (s32[2048]{0:T(1024)S(1)}, s32[2048]{0:T(1024)}, u32[]{:S(2)}) copy-start(s32[2048]{0:T(1024)} %param.8) | copy-start | bytes 24580
  8.0 28.3 %copy-start.1 = (bf16[2048,256]{1,0:T(8,128)(2,1)S(1)}, bf16[2048,256]{1,0:T(8,128)(2,1)}, u32[]{:S(2)}) copy-start(bf16[2048,256]{1,0:T(8,128)(2,1)} %user_ref.3) | copy-start | bytes 3145732
  8.0 68.9 %all-gather.2.cloned.1.call-start = ((), (), s32[]{:S(2)}) async-start(), calls=%async_computation.7 | async-start | bytes 2162688 | tf_op jit(solution)/shard_map/all_gather | solution.py:106
  11.5 24.8 %all-to-all-start = ((bf16[32,32,384]{2,1,0:T(8,128)(2,1)}), bf16[32,32,384]{2,1,0:T(8,128)(2,1)S(1)}, u32[]{:S(2)}, u32[]{:S(2)}) async-start(bf16[32,32,384]{2,1,0:T(8,128)(2,1)} %broadcast_in_dim.21), calls=%async_computation | async-start | bytes 1572864 | tf_op jit(solution)/shard_map/all_to_all | solution.py:21
  22.0 126.2 %reduce-scatter.2.cloned.1.call-start = ((), (), s32[]{:S(2)}) async-start(), calls=%async_computation.6 | async-start | bytes 2228224 | tf_op jit(solution)/shard_map/reduce_scatter | solution.py:152
Sparse Core Ops, SparseCore 0:
  12.0 64.8 all-gather.1
Sparse Core Ops, SparseCore 1:
  72.2 68.8 reduce-scatter.1
